TPU v7x, 32 devices: a whole 2x2x4 slice. The times are simulated.
32 devices in a mesh: seq: 2 (over core), batch: 16 (over z, y, x).
Axes of the slice: x: 2, y: 2, z: 4, core: 2. Of those that a mesh axis runs over, the one named last changes fastest.
Arguments:
- activations: bfloat16 [32, 1024, 768], P('batch', 'seq'), may hold values from -6 to 6
- cotangent: bfloat16 [32, 1024, 768], P('batch', 'seq'), may hold values from -6 to 6
- lengths: int32 [32], P('batch'), may hold values from 512 to 1024, as said below
- weights_qkv: bfloat16 [2, 768, 2304], replicated, may hold values from -0.21875 to 0.21875
- conv_taps: float32 [2, 2304, 3], replicated, may hold values from -3 to 3
- weights_out: bfloat16 [2, 768, 768], replicated, may hold values from -0.875 to 0.875
- weights_up: bfloat16 [2, 768, 3072], replicated, may hold values from -0.21875 to 0.21875
- weights_down: bfloat16 [2, 3072, 768], replicated, may hold values from -0.109375 to 0.109375
- norm_gains: float32 [2, 768, 2], replicated, may hold values from 0.5 to 1.5
- norm_biases: float32 [2, 768, 2], replicated, may hold values from -1.8 to 1.8
Outputs:
- block_out: bfloat16 [32, 1024, 768], P('batch', 'seq')
- grad_input: bfloat16 [32, 1024, 768], P('batch', 'seq')
- grad_qkv: float32 [2, 768, 2304], P(None, ('seq', 'batch'))
- grad_taps: float32 [2, 2304, 3], P(None, ('seq', 'batch'))
- grad_out: float32 [2, 768, 768], P(None, ('seq', 'batch'))
- grad_up: float32 [2, 768, 3072], P(None, ('seq', 'batch'))
- grad_down: float32 [2, 3072, 768], P(None, ('seq', 'batch'))
- grad_gains: float32 [2, 768, 2], P(None, ('seq', 'batch'))
- grad_biases: float32 [2, 768, 2], P(None, ('seq', 'batch'))
Inputs may be any that keep to these rules, and one draw needn't show every extreme that they name: `lengths`: each value is 1024 or 512; among the 2 sequences of one index of batch (an aligned block of 2 entries) one, chosen by the seed, has 1024.
All inputs are finite; a program needn't handle non-finite values.
Results may differ from a plain program's by a relative error of at most 0.02.
Values may be sent and summed in bfloat16 or wider, within the bound.
A program may use at most 384 MiB of HBM per device.

v0:
```python
import jax
import jax.numpy as jnp
from jax import lax
from jax.sharding import PartitionSpec as P

HEAD_DIM = 64
LAYERS = 2


def shifted(x, axis, by):
    size = lax.axis_size(axis)
    pairs = [(i, i + by) for i in range(size) if 0 <= i + by < size]
    return lax.ppermute(x, axis, pairs)


def normalize(stream):
    average = jnp.mean(stream, -1, keepdims=True)
    centered = stream - average
    scaling = lax.rsqrt(jnp.mean(centered * centered, -1, keepdims=True) + 1e-05)
    return (centered * scaling, scaling)


def norm_back(grad_norm, normed, scaling, gain):
    scaled = grad_norm * gain
    return scaling * (
        scaled
        - jnp.mean(scaled, -1, keepdims=True)
        - normed * jnp.mean(scaled * normed, -1, keepdims=True)
    )


def split_heads(block):
    return block.reshape(block.shape[0], -1, HEAD_DIM)


def masked_scores(query_seq, key_seq, length, positions):
    scores = jnp.einsum(
        "qhd,khd->hqk",
        split_heads(query_seq),
        split_heads(key_seq),
        preferred_element_type=jnp.float32,
    ) * HEAD_DIM ** (-0.5)
    key_place = jnp.arange(key_seq.shape[0], dtype=jnp.int32)
    allowed = (key_place[None, :] < length) & (
        (key_place[None, :] <= positions[:, None]) | (positions[:, None] >= length)
    )
    return jnp.where(allowed[None], scores, -1e30)


def attention_forward(queries, keys_all, values_all, lengths, positions):

    def one_sequence(items):
        query_seq, key_seq, value_seq, length = items
        scores = masked_scores(query_seq, key_seq, length, positions)
        highest = jnp.max(scores, -1, keepdims=True)
        expo = jnp.exp(scores - highest)
        totals = jnp.sum(expo, -1, keepdims=True)
        probs = (expo / totals).astype(jnp.bfloat16)
        mixed = jnp.einsum(
            "hqk,khd->qhd", probs, split_heads(value_seq), preferred_element_type=jnp.float32
        )
        log_total = (highest + jnp.log(totals))[..., 0]
        return (mixed.reshape(query_seq.shape).astype(jnp.bfloat16), log_total)

    return lax.map(one_sequence, (queries, keys_all, values_all, lengths))


def attention_backward(
    queries, keys_all, values_all, lengths, positions, log_totals, grad_attended
):

    def one_sequence(items):
        query_seq, key_seq, value_seq, length, log_total, grad_seq = items
        scores = masked_scores(query_seq, key_seq, length, positions)
        probs = jnp.exp(scores - log_total[..., None])
        grad_heads = split_heads(grad_seq)
        grad_probs = jnp.einsum(
            "qhd,khd->hqk", grad_heads, split_heads(value_seq), preferred_element_type=jnp.float32
        )
        inner = jnp.sum(probs * grad_probs, -1, keepdims=True)
        grad_scores = (probs * (grad_probs - inner)).astype(jnp.bfloat16)
        grad_query = jnp.einsum(
            "hqk,khd->qhd", grad_scores, split_heads(key_seq), preferred_element_type=jnp.float32
        ) * HEAD_DIM ** (-0.5)
        grad_key = jnp.einsum(
            "hqk,qhd->khd", grad_scores, split_heads(query_seq), preferred_element_type=jnp.float32
        ) * HEAD_DIM ** (-0.5)
        grad_value = jnp.einsum(
            "hqk,qhd->khd",
            probs.astype(jnp.bfloat16),
            grad_heads,
            preferred_element_type=jnp.float32,
        )
        return (
            grad_query.reshape(query_seq.shape),
            grad_key.reshape(key_seq.shape),
            grad_value.reshape(key_seq.shape),
        )

    return lax.map(
        one_sequence, (queries, keys_all, values_all, lengths, log_totals, grad_attended)
    )


def layer_forward(stream, lengths, positions, w_qkv, taps, w_out, w_up, w_down, gains, offsets):
    seqs_here, rows, width = stream.shape
    tokens = seqs_here * rows
    normed_one, scale_one = normalize(stream)
    attn_in = (normed_one * gains[:, 0] + offsets[:, 0]).astype(jnp.bfloat16)
    projected = jnp.dot(
        attn_in.reshape(tokens, width), w_qkv, preferred_element_type=jnp.float32
    ).reshape(seqs_here, rows, 3 * width)
    before = shifted(projected[:, rows - 2 :, :].astype(jnp.bfloat16), "seq", 1).astype(jnp.float32)
    extended = jnp.concatenate([before, projected], 1)
    conv_out = (
        taps[:, 0] * extended[:, 2:]
        + taps[:, 1] * extended[:, 1 : rows + 1]
        + taps[:, 2] * extended[:, :rows]
    )
    mixed_qkv = conv_out.astype(jnp.bfloat16)
    queries = mixed_qkv[..., :width]
    keys_here = mixed_qkv[..., width : 2 * width]
    values_here = mixed_qkv[..., 2 * width :]
    keys_all, values_all = (
        lax.all_gather(keys_here, "seq", axis=1, tiled=True),
        lax.all_gather(values_here, "seq", axis=1, tiled=True),
    )
    attended, log_totals = attention_forward(queries, keys_all, values_all, lengths, positions)
    branch = jnp.dot(attended.reshape(tokens, width), w_out, preferred_element_type=jnp.float32)
    middle = stream + branch.reshape(stream.shape)
    normed_two, scale_two = normalize(middle)
    ff_in = (normed_two * gains[:, 1] + offsets[:, 1]).astype(jnp.bfloat16).reshape(tokens, width)
    hidden_pre = jnp.dot(ff_in, w_up, preferred_element_type=jnp.float32)
    hidden = (jax.nn.relu(hidden_pre) ** 2).astype(jnp.bfloat16)
    result = middle + jnp.dot(hidden, w_down, preferred_element_type=jnp.float32).reshape(
        stream.shape
    )
    kept_keys = (keys_all, values_all)
    saved = (
        normed_one,
        scale_one,
        attn_in,
        extended,
        queries,
        kept_keys,
        attended,
        log_totals,
        normed_two,
        scale_two,
        ff_in,
        hidden_pre,
        hidden,
    )
    return (result, saved)


def layer_backward(grad_stream, lengths, positions, saved, w_qkv, taps, w_out, w_up, w_down, gains):
    (
        normed_one,
        scale_one,
        attn_in,
        extended,
        queries,
        kept_keys,
        attended,
        log_totals,
        normed_two,
        scale_two,
        ff_in,
        hidden_pre,
        hidden,
    ) = saved
    seqs_here, rows, width = grad_stream.shape
    tokens = seqs_here * rows
    grad_down_in = grad_stream.reshape(tokens, width).astype(jnp.bfloat16)
    grad_down = jnp.einsum("tf,td->fd", hidden, grad_down_in, preferred_element_type=jnp.float32)
    grad_hidden = jnp.dot(grad_down_in, w_down.T, preferred_element_type=jnp.float32)
    grad_pre = (grad_hidden * 2.0 * jax.nn.relu(hidden_pre)).astype(jnp.bfloat16)
    grad_up = jnp.einsum("td,tf->df", ff_in, grad_pre, preferred_element_type=jnp.float32)
    grad_ffin = jnp.dot(grad_pre, w_up.T, preferred_element_type=jnp.float32).reshape(
        grad_stream.shape
    )
    gain_two = jnp.sum(grad_ffin * normed_two, (0, 1))
    offset_two = jnp.sum(grad_ffin, (0, 1))
    grad_middle = grad_stream + norm_back(grad_ffin, normed_two, scale_two, gains[:, 1])
    grad_branch = grad_middle.reshape(tokens, width).astype(jnp.bfloat16)
    grad_out = jnp.einsum(
        "td,te->de",
        attended.reshape(tokens, width),
        grad_branch,
        preferred_element_type=jnp.float32,
    )
    grad_attended = jnp.dot(grad_branch, w_out.T, preferred_element_type=jnp.float32)
    grad_attended = grad_attended.astype(jnp.bfloat16).reshape(grad_stream.shape)
    keys_all, values_all = kept_keys
    grad_query, grad_key_all, grad_value_all = attention_backward(
        queries, keys_all, values_all, lengths, positions, log_totals, grad_attended
    )
    grad_key, grad_value = (
        lax.psum_scatter(
            grad_key_all.astype(jnp.bfloat16), "seq", scatter_dimension=1, tiled=True
        ).astype(jnp.float32),
        lax.psum_scatter(
            grad_value_all.astype(jnp.bfloat16), "seq", scatter_dimension=1, tiled=True
        ).astype(jnp.float32),
    )
    grad_conv = jnp.concatenate([grad_query, grad_key, grad_value], -1)
    after = shifted(grad_conv[:, :2, :].astype(jnp.bfloat16), "seq", -1).astype(jnp.float32)
    grad_ext = jnp.concatenate([grad_conv, after], 1)
    grad_proj = (
        taps[:, 0] * grad_ext[:, :rows]
        + taps[:, 1] * grad_ext[:, 1 : rows + 1]
        + taps[:, 2] * grad_ext[:, 2:]
    )
    grad_taps = jnp.stack(
        [
            jnp.sum(grad_conv * extended[:, 2:], (0, 1)),
            jnp.sum(grad_conv * extended[:, 1 : rows + 1], (0, 1)),
            jnp.sum(grad_conv * extended[:, :rows], (0, 1)),
        ],
        -1,
    )
    grad_proj_low = grad_proj.reshape(tokens, 3 * width).astype(jnp.bfloat16)
    grad_qkv = jnp.einsum(
        "td,tf->df",
        attn_in.reshape(tokens, width),
        grad_proj_low,
        preferred_element_type=jnp.float32,
    )
    grad_attn_in = jnp.dot(grad_proj_low, w_qkv.T, preferred_element_type=jnp.float32).reshape(
        grad_stream.shape
    )
    gain_one = jnp.sum(grad_attn_in * normed_one, (0, 1))
    offset_one = jnp.sum(grad_attn_in, (0, 1))
    grad_input = grad_middle + norm_back(grad_attn_in, normed_one, scale_one, gains[:, 0])
    grad_gains = jnp.stack([gain_one, gain_two], -1)
    grad_biases = jnp.stack([offset_one, offset_two], -1)
    return (
        grad_input,
        (grad_qkv, grad_taps, grad_out, grad_up, grad_down, grad_gains, grad_biases),
    )


def reduce_grads(grad_qkv, grad_taps, grad_out, grad_up, grad_down, grad_gains, grad_biases):
    part_qkv, part_taps, part_out, part_up, part_down, part_gains, part_biases = (
        lax.psum_scatter(
            grad_qkv.astype(jnp.bfloat16), "seq", scatter_dimension=0, tiled=True
        ).astype(jnp.float32),
        lax.psum_scatter(
            grad_taps.astype(jnp.bfloat16), "seq", scatter_dimension=0, tiled=True
        ).astype(jnp.float32),
        lax.psum_scatter(
            grad_out.astype(jnp.bfloat16), "seq", scatter_dimension=0, tiled=True
        ).astype(jnp.float32),
        lax.psum_scatter(
            grad_up.astype(jnp.bfloat16), "seq", scatter_dimension=0, tiled=True
        ).astype(jnp.float32),
        lax.psum_scatter(
            grad_down.astype(jnp.bfloat16), "seq", scatter_dimension=0, tiled=True
        ).astype(jnp.float32),
        lax.psum_scatter(
            grad_gains.astype(jnp.bfloat16), "seq", scatter_dimension=0, tiled=True
        ).astype(jnp.float32),
        lax.psum_scatter(
            grad_biases.astype(jnp.bfloat16), "seq", scatter_dimension=0, tiled=True
        ).astype(jnp.float32),
    )
    return (
        lax.psum_scatter(
            part_qkv.astype(jnp.bfloat16), "batch", scatter_dimension=0, tiled=True
        ).astype(jnp.float32),
        lax.psum_scatter(
            part_taps.astype(jnp.bfloat16), "batch", scatter_dimension=0, tiled=True
        ).astype(jnp.float32),
        lax.psum_scatter(
            part_out.astype(jnp.bfloat16), "batch", scatter_dimension=0, tiled=True
        ).astype(jnp.float32),
        lax.psum_scatter(
            part_up.astype(jnp.bfloat16), "batch", scatter_dimension=0, tiled=True
        ).astype(jnp.float32),
        lax.psum_scatter(
            part_down.astype(jnp.bfloat16), "batch", scatter_dimension=0, tiled=True
        ).astype(jnp.float32),
        lax.psum_scatter(
            part_gains.astype(jnp.bfloat16), "batch", scatter_dimension=0, tiled=True
        ).astype(jnp.float32),
        lax.psum_scatter(
            part_biases.astype(jnp.bfloat16), "batch", scatter_dimension=0, tiled=True
        ).astype(jnp.float32),
    )


def local(
    activations,
    cotangent,
    lengths,
    weights_qkv,
    conv_taps,
    weights_out,
    weights_up,
    weights_down,
    norm_gains,
    norm_biases,
):
    seqs_here, rows, width = activations.shape
    positions = lax.axis_index("seq") * rows + jnp.arange(rows, dtype=jnp.int32)
    stream = activations.astype(jnp.float32)
    saved_all = []
    for layer_num in range(LAYERS):
        stream, saved = layer_forward(
            stream,
            lengths,
            positions,
            weights_qkv[layer_num],
            conv_taps[layer_num],
            weights_out[layer_num],
            weights_up[layer_num],
            weights_down[layer_num],
            norm_gains[layer_num],
            norm_biases[layer_num],
        )
        saved_all.append(saved)
    block_out = stream.astype(jnp.bfloat16)
    grad_stream = cotangent.astype(jnp.float32)
    collected = []
    for layer_num in reversed(range(LAYERS)):
        grad_stream, layer_grads = layer_backward(
            grad_stream,
            lengths,
            positions,
            saved_all[layer_num],
            weights_qkv[layer_num],
            conv_taps[layer_num],
            weights_out[layer_num],
            weights_up[layer_num],
            weights_down[layer_num],
            norm_gains[layer_num],
        )
        grad_qkv, grad_taps, grad_out, grad_up, grad_down, grad_gains, grad_biases = layer_grads
        collected.append(
            reduce_grads(grad_qkv, grad_taps, grad_out, grad_up, grad_down, grad_gains, grad_biases)
        )
    collected = collected[::-1]
    stacked = [jnp.stack([member[index] for member in collected], 0) for index in range(7)]
    return (
        block_out,
        grad_stream.astype(jnp.bfloat16),
        stacked[0],
        stacked[1],
        stacked[2],
        stacked[3],
        stacked[4],
        stacked[5],
        stacked[6],
    )


def solution(mesh):
    placed = (
        P("batch", "seq", None),
        P("batch", "seq", None),
        P("batch"),
        P(),
        P(),
        P(),
        P(),
        P(),
        P(),
        P(),
    )
    return jax.shard_map(
        local,
        mesh=mesh,
        in_specs=placed,
        out_specs=(
            P("batch", "seq", None),
            P("batch", "seq", None),
            P(None, ("seq", "batch"), None),
            P(None, ("seq", "batch"), None),
            P(None, ("seq", "batch"), None),
            P(None, ("seq", "batch"), None),
            P(None, ("seq", "batch"), None),
            P(None, ("seq", "batch"), None),
            P(None, ("seq", "batch"), None),
        ),
        check_vma=False,
    )
```

profile of v0, /device:TPU:0, one launch (start us, length us, event | category | flops | bytes accessed | tf_op | source)
XLA Modules:
  0.0 2096.3 jit_solution(5132532723835882918)
XLA Ops:
  31.3 11.7 all-gather.5.cloned.1.call-done
  46.1 12.2 all-gather.7.cloned.1.call-done
  64.3 82.9 %while.56 = (s32[]{:T(128)}, bf16[2,512,768]{1,2,0:T(8,128)(2,1)}, f32[2,12,512]{2,1,0:T(8,128)S(1)}, bf16[2,1024,768]{1,2,0:T(8,128)(2,1)S(1)}, s32[2]{0:T(128)...) while((s32[]{:T(128)}, bf16[2,512,768]{1,2,0:T(8,128)(2,1)}, ...), condition=%wide.region_5.6_spmd.clone, body=%wide.region_2.5_spmd.clone.sunk | while | flops 1688072704 | bytes 198934192 | solution.py:65
  69.8 10.7 fusion.225
  80.5 12.3 fusion.226
  111.2 10.7 fusion.225
  121.9 12.3 fusion.226
  189.1 11.2 all-gather.9.cloned.1.call-done
  204.9 10.7 all-gather.11.cloned.1.call-done
  222.1 85.3 %while.57 = (s32[]{:T(128)}, bf16[2,512,768]{1,2,0:T(8,128)(2,1)}, f32[2,12,512]{2,1,0:T(8,128)}, bf16[2,1024,768]{1,2,0:T(8,128)(2,1)}, s32[2]{0:T(128)S(1)}, /...) while((s32[]{:T(128)}, bf16[2,512,768]{1,2,0:T(8,128)(2,1)}, ...), condition=%wide.region_13.14_spmd.clone, body=%wide.region_10.13_spmd.clone.sunk | while | flops 1688072704 | bytes 192626832 | solution.py:65
  228.2 10.7 fusion.232
  238.9 12.3 fusion.233
  270.7 10.7 fusion.232
  281.4 12.3 fusion.233
  321.4 11.5 multiply_convert_fusion.3
  353.2 186.6 %while.58 = (s32[]{:T(128)}, f32[2,512,768]{2,1,0:T(8,128)}, bf16[2,1024,768]{2,1,0:T(8,128)(2,1)}, bf16[2,1024,768]{2,1,0:T(8,128)(2,1)}, bf16[2,1024,768]{1,2,...) while((s32[]{:T(128)}, f32[2,512,768]{2,1,0:T(8,128)}, ...), condition=%wide.region_20.21_spmd.clone, body=%wide.region_18.20_spmd.clone.sunk | while | flops 4124439040 | bytes 292208896 | solution.py:100
  375.8 18.1 multiply_reduce_fusion.23
  393.9 16.8 multiply_convert_fusion.8
  417.5 13.0 fusion.247
  468.8 18.1 multiply_reduce_fusion.23
  486.9 16.8 multiply_convert_fusion.8
  510.5 13.0 fusion.247
  540.4 11.6 reduce-scatter.45.cloned.1.call-done
  553.6 12.6 reduce-scatter.47.cloned.1.call-done
  582.8 17.3 multiply_reduce_fusion.3
  612.2 10.3 multiply_convert_fusion.2
  622.6 11.0 multiply_reduce_fusion.10
  644.0 182.7 %while.59 = (s32[]{:T(128)}, f32[2,512,768]{2,1,0:T(8,128)}, bf16[2,1024,768]{2,1,0:T(8,128)(2,1)}, bf16[2,1024,768]{2,1,0:T(8,128)(2,1)}, bf16[2,1024,768]{1,2,...) while((s32[]{:T(128)}, f32[2,512,768]{2,1,0:T(8,128)}, ...), condition=%wide.region_29.30_spmd.clone, body=%wide.region_27.29_spmd.clone.sunk | while | flops 4124439040 | bytes 298500352 | solution.py:100
  664.7 18.1 multiply_reduce_fusion.24
  682.8 16.8 multiply_convert_fusion.9
  706.4 13.0 fusion.260
  755.8 18.1 multiply_reduce_fusion.24
  773.9 16.8 multiply_convert_fusion.9
  797.5 13.0 fusion.260
  847.6 10.7 convolution_convert_fusion.1
  910.8 18.7 multiply_reduce_fusion.6
  984.3 10.5 reduce-scatter.91.cloned.1.call-done
  995.8 11.1 reduce-scatter.87.cloned.1.call-done
  1008.0 127.6 %reduce-scatter.67.cloned.1.call-done = bf16[24,768]{1,0:T(8,128)(2,1)} async-done(((bf16[384,768]{1,0:T(8,128)(2,1)}), bf16[24,768]{1,0:T(8,128)(2,1)}) %reduce-scatter.67.cloned.1.call-update) | async-done | bytes 36880 | tf_op jit(solution)/shard_map/reduce_scatter | solution.py:275
  1135.6 125.9 %reduce-scatter.63.cloned.1.call-done = bf16[24,768]{1,0:T(8,128)(2,1)} async-done(((bf16[384,768]{1,0:T(8,128)(2,1)}), bf16[24,768]{1,0:T(8,128)(2,1)}) %reduce-scatter.63.cloned.1.call-update) | async-done | bytes 36880 | tf_op jit(solution)/shard_map/reduce_scatter | solution.py:275
  1282.5 11.0 reduce-scatter.85.cloned.1.call-done
  1294.7 77.4 %all-reduce.6 = (bf16[1152,3]{0,1:T(4,128)(2,1)S(1)}, bf16[1152,3]{0,1:T(4,128)(2,1)S(1)}, bf16[384,2]{0,1:T(2,128)(2,1)S(1)}, bf16[384,2]{0,1:T(2,128)(2,1)S(1)...) all-reduce(bf16[1152,3]{0,1:T(4,128)(2,1)S(1)} %copy.102, ...), channel_id=13, replica_groups=mesh['seq'=2,'batch'=16] {'batch'}, use_global_device_ids=true, to_apply=%region_47.48.clone | all-reduce | flops 9984 | bytes 39936
  1374.3 53.9 %reduce-scatter.83.cloned.1.call-done = bf16[96,768]{1,0:T(8,128)(2,1)} async-done(((bf16[1536,768]{1,0:T(8,128)(2,1)}), bf16[96,768]{1,0:T(8,128)(2,1)}) %reduce-scatter.83.cloned.1.call-update) | async-done | bytes 147472 | tf_op jit(solution)/shard_map/reduce_scatter | solution.py:281
  1428.2 132.9 %reduce-scatter.79.cloned.1.call-done = bf16[96,768]{1,0:T(8,128)(2,1)} async-done(((bf16[1536,768]{1,0:T(8,128)(2,1)}), bf16[96,768]{1,0:T(8,128)(2,1)}) %reduce-scatter.79.cloned.1.call-update) | async-done | bytes 147472 | tf_op jit(solution)/shard_map/reduce_scatter | solution.py:281
  1563.0 130.4 %reduce-scatter.75.cloned.1.call-done = bf16[24,3072]{1,0:T(8,128)(2,1)} async-done(((bf16[384,3072]{1,0:T(8,128)(2,1)}), bf16[24,3072]{1,0:T(8,128)(2,1)}) %reduce-scatter.75.cloned.1.call-update) | async-done | bytes 147472 | tf_op jit(solution)/shard_map/reduce_scatter | solution.py:278
  1693.4 133.1 %reduce-scatter.71.cloned.1.call-done = bf16[24,3072]{1,0:T(8,128)(2,1)} async-done(((bf16[384,3072]{1,0:T(8,128)(2,1)}), bf16[24,3072]{1,0:T(8,128)(2,1)}) %reduce-scatter.71.cloned.1.call-update) | async-done | bytes 147472 | tf_op jit(solution)/shard_map/reduce_scatter | solution.py:278
  1828.3 128.7 %reduce-scatter.59.cloned.1.call-done = bf16[24,2304]{1,0:T(8,128)(2,1)} async-done(((bf16[384,2304]{1,0:T(8,128)(2,1)}), bf16[24,2304]{1,0:T(8,128)(2,1)}) %reduce-scatter.59.cloned.1.call-update) | async-done | bytes 110608 | tf_op jit(solution)/shard_map/reduce_scatter | solution.py:269
  1957.0 130.2 %reduce-scatter.55.cloned.1.call-done = bf16[24,2304]{1,0:T(8,128)(2,1)} async-done(((bf16[384,2304]{1,0:T(8,128)(2,1)}), bf16[24,2304]{1,0:T(8,128)(2,1)}) %reduce-scatter.55.cloned.1.call-update) | async-done | bytes 110608 | tf_op jit(solution)/shard_map/reduce_scatter | solution.py:269
  (592 shorter events, 570.4 us)
Async XLA Ops:
  7.2 35.7 %all-gather.5.cloned.1.call-start = ((), (), s32[]{:S(2)}) async-start(), calls=%async_computation.26 | async-start | bytes 4718592 | tf_op jit(solution)/shard_map/all_gather | solution.py:126
  19.3 3.8 collective-permute-start
  28.6 29.7 %all-gather.7.cloned.1.call-start = ((), (), s32[]{:S(2)}) async-start(), calls=%async_computation.27 | async-start | bytes 4718592 | tf_op jit(solution)/shard_map/all_gather | solution.py:125
  29.4 170.9 %all-gather.9.cloned.1.call-start = ((), (), s32[]{:S(2)}) async-start(), calls=%async_computation.28 | async-start | bytes 4718592 | tf_op jit(solution)/shard_map/all_gather | solution.py:126
  46.1 18.2 copy-start.112
  178.2 2.9 collective-permute-start.1
  186.7 28.9 %all-gather.11.cloned.1.call-start = ((), (), s32[]{:S(2)}) async-start(), calls=%async_computation.29 | async-start | bytes 4718592 | tf_op jit(solution)/shard_map/all_gather | solution.py:125
  187.3 364.7 %reduce-scatter.45.cloned.1.call-start = ((), (), s32[]{:S(2)}) async-start(), calls=%async_computation.30 | async-start | bytes 4718592 | tf_op jit(solution)/shard_map/reduce_scatter | solution.py:200
  222.1 85.3 %copy-start.19 = (f32[2,512,768]{2,1,0:T(8,128)S(1)}, f32[2,512,768]{2,1,0:T(8,128)}, u32[]{:S(2)}) copy-start(f32[2,512,768]{2,1,0:T(8,128)} %copy-done.18) | copy-start | bytes 9437188
  310.9 30.8 %copy-start.7 = (f32[2,512,768]{2,1,0:T(8,128)}, f32[2,512,768]{2,1,0:T(8,128)S(1)}, u32[]{:S(2)}) copy-start(f32[2,512,768]{2,1,0:T(8,128)S(1)} %get-tuple-element.602) | copy-start | bytes 9437188
  311.0 30.7 %copy-start.62 = (f32[2,512]{1,0:T(2,128)}, f32[2,512]{1,0:T(2,128)S(1)}, u32[]{:S(2)}) copy-start(f32[2,512]{1,0:T(2,128)S(1)} %broadcast_multiply_fusion.8) | copy-start | bytes 12292
  311.5 30.2 %copy-start.68 = (f32[2,512]{1,0:T(2,128)}, f32[2,512]{1,0:T(2,128)S(1)}, u32[]{:S(2)}) copy-start(f32[2,512]{1,0:T(2,128)S(1)} %add_rsqrt_fusion) | copy-start | bytes 12292
  356.0 37.9 %copy-start.4 = (pred[512,1024]{1,0:T(8,128)(4,1)}, pred[512,1024]{1,0:T(8,128)(4,1)S(1)}, u32[]{:S(2)}) copy-start(pred[512,1024]{1,0:T(8,128)(4,1)S(1)} %fusion.246) | copy-start | bytes 1572868 | tf_op jit(solution)/shard_map/while
  449.0 37.9 %copy-start.4 = (pred[512,1024]{1,0:T(8,128)(4,1)}, pred[512,1024]{1,0:T(8,128)(4,1)S(1)}, u32[]{:S(2)}) copy-start(pred[512,1024]{1,0:T(8,128)(4,1)S(1)} %fusion.246) | copy-start | bytes 1572868 | tf_op jit(solution)/shard_map/while
  539.8 26.5 %reduce-scatter.47.cloned.1.call-start = ((), (), s32[]{:S(2)}) async-start(), calls=%async_computation.31 | async-start | bytes 4718592 | tf_op jit(solution)/shard_map/reduce_scatter | solution.py:203
  540.3 350.4 %reduce-scatter.49.cloned.1.call-start = ((), (), s32[]{:S(2)}) async-start(), calls=%async_computation.32 | async-start | bytes 4718592 | tf_op jit(solution)/shard_map/reduce_scatter | solution.py:200
  575.9 3.1 collective-permute-start.2
  582.8 17.3 copy-start.76
  646.8 36.0 %copy-start.5 = (pred[512,1024]{1,0:T(8,128)(4,1)}, pred[512,1024]{1,0:T(8,128)(4,1)S(1)}, u32[]{:S(2)}) copy-start(pred[512,1024]{1,0:T(8,128)(4,1)S(1)} %fusion.259) | copy-start | bytes 1572868 | tf_op jit(solution)/shard_map/while
  738.0 36.0 %copy-start.5 = (pred[512,1024]{1,0:T(8,128)(4,1)}, pred[512,1024]{1,0:T(8,128)(4,1)S(1)}, u32[]{:S(2)}) copy-start(pred[512,1024]{1,0:T(8,128)(4,1)S(1)} %fusion.259) | copy-start | bytes 1572868 | tf_op jit(solution)/shard_map/while
  826.8 66.0 %reduce-scatter.51.cloned.1.call-start = ((), (), s32[]{:S(2)}) async-start(), calls=%async_computation.33 | async-start | bytes 4718592 | tf_op jit(solution)/shard_map/reduce_scatter | solution.py:203
  827.5 114.8 %reduce-scatter.65.cloned.1.call-start = ((), (), s32[]{:S(2)}) async-start(), calls=%async_computation.40 | async-start | bytes 1769472 | tf_op jit(solution)/shard_map/reduce_scatter | solution.py:252
  832.0 110.9 %reduce-scatter.61.cloned.1.call-start = ((), (), s32[]{:S(2)}) async-start(), calls=%async_computation.38 | async-start | bytes 1769472 | tf_op jit(solution)/shard_map/reduce_scatter | solution.py:252
  836.0 120.4 %reduce-scatter.81.cloned.1.call-start = ((), (), s32[]{:S(2)}) async-start(), calls=%async_computation.48 | async-start | bytes 7077888 | tf_op jit(solution)/shard_map/reduce_scatter | solution.py:258
  846.3 110.9 %reduce-scatter.77.cloned.1.call-start = ((), (), s32[]{:S(2)}) async-start(), calls=%async_computation.46 | async-start | bytes 7077888 | tf_op jit(solution)/shard_map/reduce_scatter | solution.py:258
  858.4 99.4 %reduce-scatter.73.cloned.1.call-start = ((), (), s32[]{:S(2)}) async-start(), calls=%async_computation.44 | async-start | bytes 7077888 | tf_op jit(solution)/shard_map/reduce_scatter | solution.py:255
  869.3 89.1 %reduce-scatter.69.cloned.1.call-start = ((), (), s32[]{:S(2)}) async-start(), calls=%async_computation.42 | async-start | bytes 7077888 | tf_op jit(solution)/shard_map/reduce_scatter | solution.py:255
  880.5 78.7 %reduce-scatter.57.cloned.1.call-start = ((), (), s32[]{:S(2)}) async-start(), calls=%async_computation.36 | async-start | bytes 5308416 | tf_op jit(solution)/shard_map/reduce_scatter | solution.py:246
  890.7 81.3 %reduce-scatter.53.cloned.1.call-start = ((), (), s32[]{:S(2)}) async-start(), calls=%async_computation.34 | async-start | bytes 5308416 | tf_op jit(solution)/shard_map/reduce_scatter | solution.py:246
  902.6 3.1 collective-permute-start.3
  910.8 18.7 copy-start.74
  910.8 18.7 copy-start.88
  910.8 18.7 copy-start.95
  910.8 18.7 copy-start.101
  938.5 44.9 %reduce-scatter.95.cloned.1.call-start = ((), (), s32[]{:S(2)}) async-start(), calls=%async_computation.55 | async-start | bytes 294912
  940.0 54.8 %reduce-scatter.91.cloned.1.call-start = ((), (), s32[]{:S(2)}) async-start(), calls=%async_computation.53 | async-start | bytes 294912
  941.0 65.8 %reduce-scatter.87.cloned.1.call-start = ((), (), s32[]{:S(2)}) async-start(), calls=%async_computation.51 | async-start | bytes 884736
  942.2 193.3 %reduce-scatter.67.cloned.1.call-start = ((), (), s32[]{:S(2)}) async-start(), calls=%async_computation.41 | async-start | bytes 626688 | tf_op jit(solution)/shard_map/reduce_scatter | solution.py:275
  942.8 318.7 %reduce-scatter.63.cloned.1.call-start = ((), (), s32[]{:S(2)}) async-start(), calls=%async_computation.39 | async-start | bytes 626688 | tf_op jit(solution)/shard_map/reduce_scatter | solution.py:275
  943.6 326.9 %reduce-scatter.93.cloned.1.call-start = ((), (), s32[]{:S(2)}) async-start(), calls=%async_computation.54 | async-start | bytes 294912
  954.2 327.4 %reduce-scatter.89.cloned.1.call-start = ((), (), s32[]{:S(2)}) async-start(), calls=%async_computation.52 | async-start | bytes 294912
  955.2 338.4 %reduce-scatter.85.cloned.1.call-start = ((), (), s32[]{:S(2)}) async-start(), calls=%async_computation.50 | async-start | bytes 884736
  956.4 471.8 %reduce-scatter.83.cloned.1.call-start = ((), (), s32[]{:S(2)}) async-start(), calls=%async_computation.49 | async-start | bytes 2506752 | tf_op jit(solution)/shard_map/reduce_scatter | solution.py:281
  957.1 604.0 %reduce-scatter.79.cloned.1.call-start = ((), (), s32[]{:S(2)}) async-start(), calls=%async_computation.47 | async-start | bytes 2506752 | tf_op jit(solution)/shard_map/reduce_scatter | solution.py:281
  957.7 735.6 %reduce-scatter.75.cloned.1.call-start = ((), (), s32[]{:S(2)}) async-start(), calls=%async_computation.45 | async-start | bytes 2506752 | tf_op jit(solution)/shard_map/reduce_scatter | solution.py:278
  958.3 868.2 %reduce-scatter.71.cloned.1.call-start = ((), (), s32[]{:S(2)}) async-start(), calls=%async_computation.43 | async-start | bytes 2506752 | tf_op jit(solution)/shard_map/reduce_scatter | solution.py:278
  959.1 998.0 %reduce-scatter.59.cloned.1.call-start = ((), (), s32[]{:S(2)}) async-start(), calls=%async_computation.37 | async-start | bytes 1880064 | tf_op jit(solution)/shard_map/reduce_scatter | solution.py:269
  959.8 1127.5 %reduce-scatter.55.cloned.1.call-start = ((), (), s32[]{:S(2)}) async-start(), calls=%async_computation.35 | async-start | bytes 1880064 | tf_op jit(solution)/shard_map/reduce_scatter | solution.py:269
  (114 other events, 667.5 us)
Sparse Core Ops, SparseCore 0:
  28.7 14.1 all-gather.4
  45.0 13.2 all-gather.6
  186.9 13.3 all-gather.8
  202.3 13.2 all-gather.10
  539.9 12.0 reduce-scatter.44
  554.2 12.0 reduce-scatter.46
  826.9 12.0 reduce-scatter.48
  841.3 12.0 reduce-scatter.50
  856.2 9.8 reduce-scatter.64
  868.3 9.8 reduce-scatter.60
  880.4 13.7 reduce-scatter.80
  896.5 13.7 reduce-scatter.76
  912.7 13.7 reduce-scatter.72
  928.7 13.7 reduce-scatter.68
  944.6 12.5 reduce-scatter.56
  959.4 12.5 reduce-scatter.52
  974.6 8.7 reduce-scatter.94
  986.0 8.7 reduce-scatter.90
  997.6 9.1 reduce-scatter.86
  1012.1 123.4 reduce-scatter.66
  1140.2 121.2 reduce-scatter.62
  1263.8 6.6 reduce-scatter.92
  1272.8 8.7 reduce-scatter.88
  1284.4 9.1 reduce-scatter.84
  1298.5 129.6 reduce-scatter.82
  1433.7 127.3 reduce-scatter.78
  1565.9 127.4 reduce-scatter.74
  1699.0 127.4 reduce-scatter.70
  1831.4 125.6 reduce-scatter.58
  1961.7 125.4 reduce-scatter.54
where the time goes:
time: 2100 us
  waiting for transfers between devices  1100 us (52%)
  matrix products  480 us (23%)
  other arithmetic  230 us (11%)
  local copies, waits for them, and re-layouts  179 us (9%)
  blocking collectives  77.4 us (4%)
    reduce_scatter x2, waiting for transfers between devices, reduce_grads(): lax.psum_scatter(part_up.astype(jnp.bfloat16), 'batch', scatter_dimension...  264 us
    reduce_scatter x2, waiting for transfers between devices, reduce_grads(): lax.psum_scatter(part_qkv.astype(jnp.bfloat16), 'batch', scatter_dimensio...  259 us
    reduce_scatter x2, waiting for transfers between devices, reduce_grads(): lax.psum_scatter(part_out.astype(jnp.bfloat16), 'batch', scatter_dimensio...  254 us
    reduce_scatter x2, waiting for transfers between devices, reduce_grads(): lax.psum_scatter(part_down.astype(jnp.bfloat16), 'batch', scatter_dimensi...  187 us
    dot_general x8, matrix products, masked_scores(): jnp.einsum('qhd,khd->hqk', split_heads(query_seq), split_heads(key_seq),...  83.1 us
    unnamed x1, blocking collectives  77.4 us
    dot_general x4, matrix products, one_sequence(): jnp.einsum('qhd,khd->hqk', grad_heads, split_heads(value_seq), preferred_...  72.6 us
    convert_element_type x4, other arithmetic, one_sequence(): grad_scores = (probs * (grad_probs - inner)).astype(jnp.bfloat16)  67.3 us
  transfers between devices with their start and end apart: 34, of which 24 were waited for; matrix products, arithmetic and copies ran while one was open for 8% of the time, Pallas kernels for 0%

commit v1 on v0

--- a/solution.py
+++ b/solution.py
@@ -1,6 +1,10 @@
+import functools
+
 import jax
 import jax.numpy as jnp
 from jax import lax
+from jax.experimental import pallas as pl
+from jax.experimental.pallas import tpu as pltpu
 from jax.sharding import PartitionSpec as P
 
 HEAD_DIM = 64
@@ -355,7 +359,552 @@
     )
 
 
+TILE = 256
+LANES = 128
+MIB = 2**20
+
+
+def dot_nt(left, right):
+    return lax.dot_general(
+        left, right, (((1,), (1,)), ((), ())), preferred_element_type=jnp.float32
+    )
+
+
+def dot_nn(left, right):
+    return lax.dot_general(
+        left, right, (((1,), (0,)), ((), ())), preferred_element_type=jnp.float32
+    )
+
+
+def dot_tn(left, right):
+    return lax.dot_general(
+        left, right, (((0,), (0,)), ((), ())), preferred_element_type=jnp.float32
+    )
+
+
+def head_lanes(head):
+    lane = lax.broadcasted_iota(jnp.int32, (1, LANES), 1)
+    return (lane >= head * HEAD_DIM) & (lane < (head + 1) * HEAD_DIM)
+
+
+def causal_tile():
+    keys = lax.broadcasted_iota(jnp.int32, (TILE, TILE), 0)
+    queries = lax.broadcasted_iota(jnp.int32, (TILE, TILE), 1)
+    return keys <= queries
+
+
+def attend_kernel(length_ref, conv_ref, out_ref, log_ref):
+    cap = conv_ref.shape[2]
+    whole = length_ref[pl.program_id(0)] == cap
+    queries = conv_ref[0, 0]
+    keys = conv_ref[0, 1] * jnp.bfloat16(HEAD_DIM**-0.5)
+    keys = [jnp.where(head_lanes(head), keys, jnp.bfloat16(0)) for head in range(2)]
+    values_t = conv_ref[0, 2].T
+
+    def query_block(block, key_count, diagonal):
+        rows = slice(block * TILE, (block + 1) * TILE)
+        mixed = []
+        for head in range(2):
+            below = key_count - TILE if diagonal else key_count
+            parts = []
+            if below:
+                parts.append(dot_nt(keys[head][:below], queries[rows]))
+            if diagonal:
+                tile = dot_nt(keys[head][below:key_count], queries[rows])
+                parts.append(jnp.where(causal_tile(), tile, -1e30))
+            highest = functools.reduce(
+                jnp.maximum, [jnp.max(part, 0, keepdims=True) for part in parts]
+            )
+            expo = [jnp.exp(part - highest) for part in parts]
+            total = sum(jnp.sum(part, 0, keepdims=True) for part in expo)
+            value_head = values_t[head * HEAD_DIM : (head + 1) * HEAD_DIM]
+            got, at = None, 0
+            for part in expo:
+                size = part.shape[0]
+                term = dot_nn(value_head[:, at : at + size], part.astype(jnp.bfloat16))
+                got = term if got is None else got + term
+                at += size
+            mixed.append(got / total)
+            log_ref[0, 0, head : head + 1, rows] = highest + jnp.log(total)
+        out_ref[0, rows, :] = jnp.concatenate(mixed, 0).T.astype(jnp.bfloat16)
+
+    blocks = cap // TILE
+    for block in range(blocks // 2):
+        query_block(block, (block + 1) * TILE, True)
+
+    @pl.when(whole)
+    def _():
+        for block in range(blocks // 2, blocks):
+            query_block(block, (block + 1) * TILE, True)
+
+    @pl.when(jnp.logical_not(whole))
+    def _():
+        for block in range(blocks // 2, blocks):
+            query_block(block, cap // 2, False)
+
+
+def attend(mixed, lengths):
+    seqs, _, cap, width = mixed.shape
+    pairs = width // LANES
+    return pl.pallas_call(
+        attend_kernel,
+        grid_spec=pltpu.PrefetchScalarGridSpec(
+            num_scalar_prefetch=1,
+            grid=(seqs, pairs),
+            in_specs=[pl.BlockSpec((1, 3, cap, LANES), lambda s, p, n: (s, 0, 0, p))],
+            out_specs=[
+                pl.BlockSpec((1, cap, LANES), lambda s, p, n: (s, 0, p)),
+                pl.BlockSpec((1, 1, 2, cap), lambda s, p, n: (s, p, 0, 0)),
+            ],
+        ),
+        out_shape=[
+            jax.ShapeDtypeStruct((seqs, cap, width), jnp.bfloat16),
+            jax.ShapeDtypeStruct((seqs, pairs, 2, cap), jnp.float32),
+        ],
+        compiler_params=pltpu.CompilerParams(vmem_limit_bytes=48 * MIB),
+        cost_estimate=pl.CostEstimate(
+            flops=30_000_000_000, bytes_accessed=8_000_000, transcendentals=8_000_000
+        ),
+        name="attend",
+    )(lengths, mixed)
+
+
+def attend_back_kernel(
+    length_ref,
+    conv_ref,
+    proj_ref,
+    grad_ref,
+    out_ref,
+    log_ref,
+    taps_ref,
+    back_ref,
+    grad_taps_ref,
+    query_t_acc,
+    shift_acc,
+):
+    cap = conv_ref.shape[2]
+    whole = length_ref[pl.program_id(0)] == cap
+    factor = jnp.bfloat16(HEAD_DIM**-0.5)
+    queries = conv_ref[0, 0] * factor
+    grads = grad_ref[0]
+    keys_t = (conv_ref[0, 1] * factor).T
+    product_t = (grads.astype(jnp.float32) * out_ref[0].astype(jnp.float32)).T
+    inner = [
+        jnp.sum(product_t[head * HEAD_DIM : (head + 1) * HEAD_DIM], 0, keepdims=True)
+        for head in range(2)
+    ]
+    query_t_acc[...] = jnp.zeros_like(query_t_acc)
+    shift_acc[:, pl.ds(cap, 8), :] = jnp.zeros((3, 8, LANES), jnp.float32)
+
+    def key_block(block):
+        start = block * TILE
+        rows = slice(start, start + TILE)
+        first = head_lanes(0)
+        grad_key, grad_value = [], []
+        for head in range(2):
+            key_head = jnp.where(head_lanes(head), conv_ref[0, 1, rows, :], jnp.bfloat16(0))
+            value_head = jnp.where(head_lanes(head), conv_ref[0, 2, rows, :], jnp.bfloat16(0))
+            lanes = slice(head * HEAD_DIM, (head + 1) * HEAD_DIM)
+            logs = log_ref[0, 0, head : head + 1, :]
+            key_sum = value_sum = None
+            for size, at in ((TILE, start), (cap - start - TILE, start + TILE)):
+                if size == 0:
+                    continue
+                cols = slice(at, at + size)
+                probs = jnp.exp(dot_nt(key_head, queries[cols]) - logs[:, cols])
+                if at == start:
+                    probs = jnp.where(causal_tile(), probs, 0.0)
+                grad_probs = dot_nt(value_head, grads[cols])
+                scores = (probs * (grad_probs - inner[head][:, cols])).astype(jnp.bfloat16)
+                value_term = dot_nn(probs.astype(jnp.bfloat16), grads[cols])
+                key_term = dot_nn(scores, queries[cols])
+                key_sum = key_term if key_sum is None else key_sum + key_term
+                value_sum = value_term if value_sum is None else value_sum + value_term
+                query_t_acc[lanes, cols] += dot_nn(keys_t[lanes, rows], scores)
+            grad_key.append(key_sum)
+            grad_value.append(value_sum)
+        shift_acc[1, rows, :] = jnp.where(first, grad_key[0], grad_key[1])
+        shift_acc[2, rows, :] = jnp.where(first, grad_value[0], grad_value[1])
+
+    blocks = cap // TILE
+    for block in range(blocks // 2):
+        key_block(block)
+
+    @pl.when(whole)
+    def _():
+        for block in range(blocks // 2, blocks):
+            key_block(block)
+
+    @pl.when(jnp.logical_not(whole))
+    def _():
+        shift_acc[1:, cap // 2 : cap, :] = jnp.zeros((2, cap // 2, LANES), jnp.float32)
+
+    shift_acc[0, :cap, :] = query_t_acc[...].T
+    for kind in range(3):
+        proj = proj_ref[0, kind].astype(jnp.float32)
+        total = 0.0
+        for lag in range(3):
+            moved = shift_acc[kind, lag : lag + cap, :]
+            total = total + taps_ref[kind, lag : lag + 1, :] * moved
+            grad_taps_ref[0, kind, lag : lag + 1, :] = jnp.sum(moved * proj, 0, keepdims=True)
+        back_ref[0, kind] = total.astype(jnp.bfloat16)
+
+
+def attend_back(mixed, proj, grad, out, logs, taps, lengths):
+    seqs, _, cap, width = mixed.shape
+    pairs = width // LANES
+    triple = pl.BlockSpec((1, 3, cap, LANES), lambda s, p, n: (s, 0, 0, p))
+    single = pl.BlockSpec((1, cap, LANES), lambda s, p, n: (s, 0, p))
+    return pl.pallas_call(
+        attend_back_kernel,
+        grid_spec=pltpu.PrefetchScalarGridSpec(
+            num_scalar_prefetch=1,
+            grid=(seqs, pairs),
+            in_specs=[
+                triple,
+                triple,
+                single,
+                single,
+                pl.BlockSpec((1, 1, 2, cap), lambda s, p, n: (s, p, 0, 0)),
+                pl.BlockSpec((3, 3, LANES), lambda s, p, n: (0, 0, p)),
+            ],
+            out_specs=[
+                triple,
+                pl.BlockSpec((1, 3, 3, LANES), lambda s, p, n: (s, 0, 0, p)),
+            ],
+            scratch_shapes=[
+                pltpu.VMEM((LANES, cap), jnp.float32),
+                pltpu.VMEM((3, cap + 8, LANES), jnp.float32),
+            ],
+        ),
+        out_shape=[
+            jax.ShapeDtypeStruct(mixed.shape, jnp.bfloat16),
+            jax.ShapeDtypeStruct((seqs, 3, 3, width), jnp.float32),
+        ],
+        compiler_params=pltpu.CompilerParams(vmem_limit_bytes=48 * MIB),
+        cost_estimate=pl.CostEstimate(
+            flops=70_000_000_000, bytes_accessed=16_000_000, transcendentals=8_000_000
+        ),
+        name="attend_back",
+    )(lengths, mixed, proj, grad, out, logs, taps)
+
+
+def weight_grad_kernel(place_ref, left_ref, right_ref, out_ref):
+    parts, rows, _ = out_ref.shape
+    step = max(1, 512 // rows)
+    while parts % step:
+        step -= 1
+    for at in range(0, parts, step):
+        product = dot_tn(left_ref[:, at * rows : (at + step) * rows], right_ref[...])
+        for part in range(step):
+            out_ref[place_ref[at + part]] = product[part * rows : (part + 1) * rows].astype(
+                jnp.bfloat16
+            )
+
+
+def weight_grad(left, right, place, columns):
+    tokens, rows = left.shape
+    width = right.shape[1]
+    parts = place.shape[0]
+    return pl.pallas_call(
+        weight_grad_kernel,
+        grid_spec=pltpu.PrefetchScalarGridSpec(
+            num_scalar_prefetch=1,
+            grid=(width // columns,),
+            in_specs=[
+                pl.BlockSpec((tokens, rows), lambda i, n: (0, 0)),
+                pl.BlockSpec((tokens, columns), lambda i, n: (0, i)),
+            ],
+            out_specs=pl.BlockSpec((parts, rows // parts, columns), lambda i, n: (0, 0, i)),
+        ),
+        out_shape=jax.ShapeDtypeStruct((parts, rows // parts, width), jnp.bfloat16),
+        compiler_params=pltpu.CompilerParams(vmem_limit_bytes=48 * MIB),
+        cost_estimate=pl.CostEstimate(
+            flops=2 * tokens * rows * width,
+            bytes_accessed=2 * (tokens * (rows + width) + rows * width),
+            transcendentals=0,
+        ),
+        name="weight_grad",
+    )(place, left, right)
+
+
+def swap_core(x):
+    return lax.ppermute(x, "seq", [(0, 1), (1, 0)])
+
+
+def stage_pairs(stage, groups):
+    low = groups.bit_length() - 1
+    order = list(range(low))
+    other = [1, 0] + order[2:] if low > 1 else order
+    pairs = []
+    for core, bits in enumerate((order, other)):
+        for group in range(groups):
+            pairs.append((core * groups + group, core * groups + (group ^ (1 << bits[stage]))))
+    return pairs
+
+
+def shard_places(core, group, groups):
+    low = groups.bit_length() - 1
+    shard = jnp.arange(groups, dtype=jnp.int32)
+    place = jnp.zeros((groups,), jnp.int32)
+    for stage in range(low):
+        bit = stage
+        if low > 1 and stage < 2:
+            bit = jnp.where(core == 0, stage, 1 - stage)
+        same = ((shard >> bit) & 1) == ((group >> bit) & 1)
+        place = place * 2 + same.astype(jnp.int32)
+    return place
+
+
+def sum_over_groups(halves, groups):
+    stages = groups.bit_length() - 1
+    for stage in range(stages):
+        count = halves.shape[0] // 2
+        got = lax.ppermute(halves[:count], ("seq", "batch"), stage_pairs(stage, groups))
+        halves = (halves[count:].astype(jnp.float32) + got.astype(jnp.float32)).astype(
+            jnp.bfloat16 if stage < stages - 1 else jnp.float32
+        )
+    return halves[0]
+
+
+def local_pair(
+    activations,
+    cotangent,
+    lengths,
+    weights_qkv,
+    conv_taps,
+    weights_out,
+    weights_up,
+    weights_down,
+    norm_gains,
+    norm_biases,
+):
+    seqs, rows, width = activations.shape
+    tokens = seqs * rows
+    cap = 2 * rows
+    half = width // 2
+    core = lax.axis_index("seq")
+    group = lax.axis_index("batch")
+    groups = lax.axis_size("batch")
+    place_by_core = [shard_places(c, group, groups) for c in range(2)]
+    place_own = jnp.where(core == 0, place_by_core[0], place_by_core[1])
+    place_other = jnp.where(core == 0, place_by_core[1], place_by_core[0])
+    place_all = jnp.where(
+        core == 0,
+        jnp.concatenate([place_own + groups, place_other]),
+        jnp.concatenate([place_other, place_own + groups]),
+    )
+
+    def whole_tokens(own):
+        other = swap_core(own)
+        return jnp.concatenate(
+            [jnp.where(core == 0, own, other), jnp.where(core == 0, other, own)], 1
+        )
+
+    def own_tokens(x):
+        return lax.dynamic_slice_in_dim(x, core * rows, rows, 1)
+
+    def other_tokens(x):
+        return lax.dynamic_slice_in_dim(x, (1 - core) * rows, rows, 1)
+
+    def layer_weights(layer):
+        w_qkv = lax.dynamic_slice_in_dim(
+            weights_qkv[layer].reshape(width, 3, width), core * half, half, 2
+        )
+        taps = lax.dynamic_slice_in_dim(
+            conv_taps[layer].reshape(3, width, 3), core * half, half, 1
+        ).transpose(0, 2, 1)
+        w_out_rows = lax.dynamic_slice_in_dim(weights_out[layer], core * half, half, 0)
+        return w_qkv, taps, w_out_rows
+
+    def forward(stream, layer):
+        w_qkv, taps, _ = layer_weights(layer)
+        gains, offsets = norm_gains[layer], norm_biases[layer]
+        normed_one, scale_one = normalize(stream)
+        attn_in = whole_tokens((normed_one * gains[:, 0] + offsets[:, 0]).astype(jnp.bfloat16))
+        proj = jnp.einsum("std,dgc->sgtc", attn_in, w_qkv, preferred_element_type=jnp.float32)
+        padded = jnp.pad(proj, ((0, 0), (0, 0), (2, 0), (0, 0)))
+        mixed = (
+            taps[:, 0][:, None] * proj
+            + taps[:, 1][:, None] * padded[:, :, 1:-1]
+            + taps[:, 2][:, None] * padded[:, :, :-2]
+        ).astype(jnp.bfloat16)
+        out_heads, logs = attend(mixed, lengths)
+        got = swap_core(other_tokens(out_heads))
+        kept = own_tokens(out_heads)
+        out_own = jnp.concatenate(
+            [jnp.where(core == 0, kept, got), jnp.where(core == 0, got, kept)], 2
+        )
+        middle = stream + jnp.einsum(
+            "std,de->ste", out_own, weights_out[layer], preferred_element_type=jnp.float32
+        )
+        normed_two, scale_two = normalize(middle)
+        ff_in = (normed_two * gains[:, 1] + offsets[:, 1]).astype(jnp.bfloat16)
+        pre = jnp.einsum("std,df->stf", ff_in, weights_up[layer], preferred_element_type=jnp.float32)
+        positive = jnp.maximum(pre, 0.0)
+        hidden = (positive * positive).astype(jnp.bfloat16)
+        result = middle + jnp.einsum(
+            "stf,fd->std", hidden, weights_down[layer], preferred_element_type=jnp.float32
+        )
+        saved = (
+            normed_one,
+            scale_one,
+            attn_in,
+            proj.astype(jnp.bfloat16),
+            mixed,
+            out_heads,
+            logs,
+            normed_two,
+            scale_two,
+            ff_in,
+            positive.astype(jnp.bfloat16),
+            hidden,
+        )
+        return result, saved
+
+    def backward(grad, layer, saved):
+        (
+            normed_one,
+            scale_one,
+            attn_in,
+            proj,
+            mixed,
+            out_heads,
+            logs,
+            normed_two,
+            scale_two,
+            ff_in,
+            positive,
+            hidden,
+        ) = saved
+        w_qkv, taps, w_out_rows = layer_weights(layer)
+        gains = norm_gains[layer]
+        grad_low = grad.astype(jnp.bfloat16)
+        down = weight_grad(
+            hidden.reshape(tokens, -1), grad_low.reshape(tokens, width), place_all, 384
+        )
+        grad_hidden = jnp.einsum(
+            "std,fd->stf", grad_low, weights_down[layer], preferred_element_type=jnp.float32
+        )
+        grad_pre = (grad_hidden * 2.0 * positive.astype(jnp.float32)).astype(jnp.bfloat16)
+        up = weight_grad(ff_in.reshape(tokens, width), grad_pre.reshape(tokens, -1), place_all, 768)
+        grad_ffin = jnp.einsum(
+            "stf,df->std", grad_pre, weights_up[layer], preferred_element_type=jnp.float32
+        )
+        gain_two = jnp.sum(grad_ffin * normed_two, (0, 1))
+        offset_two = jnp.sum(grad_ffin, (0, 1))
+        grad_middle = grad + norm_back(grad_ffin, normed_two, scale_two, gains[:, 1])
+        grad_branch = whole_tokens(grad_middle.astype(jnp.bfloat16))
+        grad_heads = jnp.einsum(
+            "ste,de->std", grad_branch, w_out_rows, preferred_element_type=jnp.float32
+        ).astype(jnp.bfloat16)
+        out = weight_grad(
+            out_heads.reshape(2 * tokens, half),
+            grad_branch.reshape(2 * tokens, width),
+            place_own,
+            384,
+        )
+        grad_proj, grad_taps = attend_back(mixed, proj, grad_heads, out_heads, logs, taps, lengths)
+        grad_taps = jnp.sum(grad_taps, 0)
+        qkv = weight_grad_three(
+            attn_in.reshape(2 * tokens, width), grad_proj, place_all
+        )
+        partial = jnp.einsum(
+            "sgtc,dgc->std", grad_proj, w_qkv, preferred_element_type=jnp.float32
+        )
+        grad_attn_in = own_tokens(partial) + swap_core(
+            other_tokens(partial).astype(jnp.bfloat16)
+        ).astype(jnp.float32)
+        gain_one = jnp.sum(grad_attn_in * normed_one, (0, 1))
+        offset_one = jnp.sum(grad_attn_in, (0, 1))
+        grad_input = grad_middle + norm_back(grad_attn_in, normed_one, scale_one, gains[:, 0])
+        norms = jnp.stack(
+            [jnp.stack([gain_one, gain_two], -1), jnp.stack([offset_one, offset_two], -1)]
+        )
+        return grad_input, (down, up, out, qkv, grad_taps, norms)
+
+    def weight_grad_three(left, grad_proj, place):
+        parts = [
+            weight_grad(left, grad_proj[:, kind].reshape(2 * tokens, half), place, half)
+            for kind in range(3)
+        ]
+        return jnp.stack(parts, 2)
+
+    def add_core(both):
+        return (
+            both[groups:].astype(jnp.float32) + swap_core(both[:groups]).astype(jnp.float32)
+        ).astype(jnp.bfloat16)
+
+    def reduce_layer(parts):
+        down, up, out, qkv, grad_taps, norms = parts
+        down = sum_over_groups(add_core(down), groups)
+        up = sum_over_groups(add_core(up), groups)
+        out = sum_over_groups(out, groups)
+        got, kept = swap_core(qkv[:groups]), qkv[groups:]
+        qkv = jnp.concatenate(
+            [jnp.where(core == 0, kept, got), jnp.where(core == 0, got, kept)], 3
+        )
+        qkv = sum_over_groups(qkv.reshape(groups, qkv.shape[1], -1), groups)
+        return down, up, out, qkv, grad_taps, norms
+
+    stream = activations.astype(jnp.float32)
+    kept = []
+    for layer in range(LAYERS):
+        stream, saved = forward(stream, layer)
+        kept.append(saved)
+    grad = cotangent.astype(jnp.float32)
+    reduced = [None] * LAYERS
+    for layer in reversed(range(LAYERS)):
+        grad, parts = backward(grad, layer, kept[layer])
+        reduced[layer] = reduce_layer(parts)
+    down, up, out, qkv = (jnp.stack([layer[i] for layer in reduced]) for i in range(4))
+    taps_all = []
+    for layer in range(LAYERS):
+        mine = reduced[layer][4]
+        zero = jnp.zeros_like(mine)
+        wide = jnp.concatenate(
+            [jnp.where(core == 0, mine, zero), jnp.where(core == 0, zero, mine)], 2
+        )
+        taps_all.append(wide.transpose(0, 2, 1).reshape(3 * width, 3))
+    small = jnp.concatenate(
+        [
+            jnp.stack(taps_all).reshape(LAYERS, 2 * groups, -1),
+            jnp.stack([layer[5][0] for layer in reduced]).reshape(LAYERS, 2 * groups, -1),
+            jnp.stack([layer[5][1] for layer in reduced]).reshape(LAYERS, 2 * groups, -1),
+        ],
+        2,
+    ).transpose(1, 0, 2)
+    mine = lax.dynamic_slice_in_dim(small, core * groups, groups, 0)
+    theirs = lax.dynamic_slice_in_dim(small, (1 - core) * groups, groups, 0)
+    mine = mine + swap_core(theirs)
+    size, step = groups, groups // 2
+    while step:
+        low = (group // step) % 2
+        send = lax.dynamic_slice_in_dim(mine, (1 - low) * step, step, 0)
+        got = lax.ppermute(send, "batch", [(i, i ^ step) for i in range(groups)])
+        mine = lax.dynamic_slice_in_dim(mine, low * step, step, 0) + got
+        step //= 2
+    mine = mine[0]
+    n_taps = 3 * width * 3 // (2 * groups)
+    n_norm = width * 2 // (2 * groups)
+    grad_taps = mine[:, :n_taps].reshape(LAYERS, -1, 3)
+    grad_gains = mine[:, n_taps : n_taps + n_norm].reshape(LAYERS, -1, 2)
+    grad_biases = mine[:, n_taps + n_norm :].reshape(LAYERS, -1, 2)
+    return (
+        stream.astype(jnp.bfloat16),
+        grad.astype(jnp.bfloat16),
+        qkv,
+        grad_taps,
+        out,
+        up,
+        down,
+        grad_gains,
+        grad_biases,
+    )
+
+
 def solution(mesh):
+    chosen = local_pair if mesh.shape["seq"] == 2 else local
     placed = (
         P("batch", "seq", None),
         P("batch", "seq", None),
@@ -369,7 +918,7 @@
         P(),
     )
     return jax.shard_map(
-        local,
+        chosen,
         mesh=mesh,
         in_specs=placed,
         out_specs=(

time: 2100 us -> 609 us (0.29)
  waiting for transfers between devices: 1100 us -> 89.3 us
  matrix products: 480 us -> 104 us
  Pallas kernels: 0 us -> 185 us
  other arithmetic: 230 us -> 85.8 us
  local copies, waits for them, and re-layouts: 179 us -> 87.6 us
  blocking collectives: 77.4 us -> 0 us
  starting transfers between devices: 8.72 us -> 49.6 us
    reduce_scatter x20 -> x0, waiting for transfers between devices: 997 us -> none  [the longest x2 264 us: reduce_grads(): lax.psum_scatter(part_up.astype(jnp.bfloat16), 'batch', scatter_dimension...]
    dot_general x52 -> x16, matrix products: 480 us -> 104 us  [the longest x2 20.3 us: backward(): jnp.einsum('std,fd->stf', grad_low, weights_down[layer], preferred_elemen...]
    pallas_call x0 -> x16, Pallas kernels: none -> 185 us  [the longest x2 75.3 us: attend_back(): pl.pallas_call(attend_back_kernel, grid_spec=pltpu.PrefetchScalarGridSpec...]
    ppermute x4 -> x51, waiting for transfers between devices: 4.27 us -> 89.3 us  [the longest x32 79.2 us: sum_over_groups(): lax.ppermute(halves[:count], ('seq', 'batch'), stage_pairs(stage, groups))]
    reduce_sum x6 -> x4, other arithmetic: 85.2 us -> 5.88 us  [the longest x2 5.85 us: backward(): gain_one = jnp.sum(grad_attn_in * normed_one, (0, 1))]
    unnamed x1 -> x0, blocking collectives: 77.4 us -> none
    unnamed x36 -> x0, waiting for transfers between devices: 54.3 us -> none
    dynamic_slice x36 -> x7, local copies, waits for them, and re-layouts: 50.6 us -> 1.19 us  [the longest x2 1.13 us: other_tokens(): return lax.dynamic_slice_in_dim(x, (1 - core) * rows, rows, 1)]
  transfers between devices with their start and end apart: 34 -> 51, of which waited for: 24 -> 22; matrix products, arithmetic and copies ran while one was open for 8% -> 29% of each run, Pallas kernels for 0% -> 21%
where the time goes in v1:
time: 609 us; the launch traced here: 605 us
  Pallas kernels  185 us (30%)
  matrix products  104 us (17%)
  waiting for transfers between devices  89.3 us (15%)
  local copies, waits for them, and re-layouts  87.6 us (14%)
  other arithmetic  85.8 us (14%)
  starting transfers between devices  49.6 us (8%)
    ppermute x32, waiting for transfers between devices, sum_over_groups(): lax.ppermute(halves[:count], ('seq', 'batch'), stage_pairs(stage, groups))  79.2 us
    pallas_call x2, Pallas kernels, attend_back(): pl.pallas_call(attend_back_kernel, grid_spec=pltpu.PrefetchScalarGridSpec...  75.3 us
    pallas_call x12, Pallas kernels, weight_grad(): pl.pallas_call(weight_grad_kernel, grid_spec=pltpu.PrefetchScalarGridSpec...  62.5 us
    pallas_call x2, Pallas kernels, attend(): pl.pallas_call(attend_kernel, grid_spec=pltpu.PrefetchScalarGridSpec(num_...  47.3 us
    ppermute x32, starting transfers between devices, sum_over_groups(): lax.ppermute(halves[:count], ('seq', 'batch'), stage_pairs(stage, groups))  42 us
    dot_general x2, matrix products, backward(): jnp.einsum('std,fd->stf', grad_low, weights_down[layer], preferred_elemen...  20.3 us
    dot_general x2, matrix products, backward(): jnp.einsum('stf,df->std', grad_pre, weights_up[layer], preferred_element_...  19.1 us
    slice x3, local copies, waits for them, and re-layouts, layer_weights(): weights_qkv[layer].reshape(width, 3, width)  18.5 us
  transfers between devices with their start and end apart: 51, of which 22 were waited for; matrix products, arithmetic and copies ran while one was open for 29% of the time, Pallas kernels for 21%

profile of v1, /device:TPU:0, one launch (start us, length us, event | category | flops | bytes accessed | tf_op | source)
XLA Modules:
  0.0 604.8 jit_solution(2614252696849978451)
XLA Ops:
  6.6 6.4 %fusion.88 = (bf16[1,768,2304]{2,1,0:T(8,128)(2,1)}, bf16[1,768,2304]{2,1,0:T(8,128)(2,1)}) fusion(bf16[2,768,2304]{2,1,0:T(8,128)(2,1)} %param.13), kind=kLoop, calls=%fused_computation.273 | loop fusion | bytes 14155776 | tf_op jit(solution)/shard_map/slice | solution.py:712
  13.0 6.0 copy.47
  21.6 4.4 convolution_bitcast_fusion.1
  26.1 6.2 %fusion.86 = (bf16[2,3,1024,384]{3,2,1,0:T(8,128)(2,1)}, bf16[2,3,1024,384]{3,2,1,0:T(8,128)(2,1)}) fusion(f32[2,3,1024,384]{3,2,1,0:T(8,128)S(1)} %convolution_bitcast_fusion.1, f32[3,384]{1,0:T(4,128)S(1)} %bitcast.232, f32[3,384]{1,0:T(4,128)S(1)} %bitcast.233, f32[3,384]{1,0:T(4,128)S(1)} %bitcast.231), kind=kLoop, calls=%fused_computation.271 | loop fusion | flops 16515072 | bytes 18888192 | tf_op jit(solution)/shard_map/convert_element_type | solution.py:753
  32.3 23.6 %attend.2 = (bf16[2,1024,384]{2,1,0:T(8,128)(2,1)S(1)}, f32[2,3,2,1024]{3,2,1,0:T(2,128)S(1)}) custom-call(s32[2]{0:T(128)S(1)} %copy-done.17, bf16[2,3,1024,384]{3,2,1,0:T(8,128)(2,1)} %get-tuple-element.87.conv_ref), custom_call_target="tpu_custom_call" | custom-call | flops 30000001024 | bytes 8000000 | tf_op jit(solution)/shard_map/attend/pallas_call | solution.py:449
  66.0 8.0 %multiply_convert_fusion.3 = (bf16[2,512,3072]{2,1,0:T(8,128)(2,1)}, bf16[2,512,3072]{2,1,0:T(8,128)(2,1)}) fusion(bf16[2,512,768]{2,1,0:T(8,128)(2,1)S(1)} %add_convert_fusion.9, bf16[2,768,3072]{2,1,0:T(8,128)(2,1)S(1)} %bitcast.239), kind=kOutput, calls=%fused_computation.3 | convolution fusion | flops 4844421120 | bytes 18874368 | tf_op jit(solution)/shard_map/std,df->stf/dot_general | solution.py:743
  74.1 7.4 %fusion.97 = (f32[2,512]{1,0:T(2,128)S(1)}, f32[2,512,768]{2,1,0:T(8,128)S(1)}) fusion(f32[2,512,768]{2,1,0:T(8,128)S(1)} %get-tuple-element.139, bf16[2,512,3072]{2,1,0:T(8,128)(2,1)} %get-tuple-element.140, bf16[2,3072,768]{2,1,0:T(8,128)(2,1)S(1)} %bitcast.237), kind=kOutput, calls=%fused_computation.282 | convolution fusion | flops 4833410048 | bytes 17305600 | tf_op jit(solution)/shard_map/stf,fd->std/dot_general | solution.py:746
  83.9 6.2 %copy.50 = bf16[1,768,2304]{1,2,0:T(8,128)(2,1)} copy(bf16[1,768,2304]{2,1,0:T(8,128)(2,1)} %get-tuple-element.90) | data formatting | bytes 7077888 | tf_op jit(solution)/shard_map/slice | solution.py:712
  92.8 4.3 convolution_bitcast_fusion
  97.1 6.2 %fusion.87 = (bf16[2,3,1024,384]{3,2,1,0:T(8,128)(2,1)}, bf16[2,3,1024,384]{3,2,1,0:T(8,128)(2,1)}) fusion(f32[2,3,1024,384]{3,2,1,0:T(8,128)S(1)} %convolution_bitcast_fusion, f32[3,384]{1,0:T(4,128)S(1)} %bitcast.229, f32[3,384]{1,0:T(4,128)S(1)} %bitcast.230, f32[3,384]{1,0:T(4,128)S(1)} %bitcast.228), kind=kLoop, calls=%fused_computation.272 | loop fusion | flops 16515072 | bytes 18888192 | tf_op jit(solution)/shard_map/convert_element_type | solution.py:753
  103.3 23.7 %attend.3 = (bf16[2,1024,384]{2,1,0:T(8,128)(2,1)S(1)}, f32[2,3,2,1024]{3,2,1,0:T(2,128)S(1)}) custom-call(s32[2]{0:T(128)S(1)} %copy-done.17, bf16[2,3,1024,384]{3,2,1,0:T(8,128)(2,1)} %get-tuple-element.89.conv_ref), custom_call_target="tpu_custom_call" | custom-call | flops 30000001024 | bytes 8000000 | tf_op jit(solution)/shard_map/attend/pallas_call | solution.py:449
  136.9 9.4 %multiply_convert_fusion.2 = (bf16[2,512,3072]{2,1,0:T(8,128)(2,1)}, bf16[2,512,3072]{2,1,0:T(8,128)(2,1)S(1)}) fusion(bf16[2,512,768]{2,1,0:T(8,128)(2,1)S(1)} %add_convert_fusion.7, bf16[2,768,3072]{2,1,0:T(8,128)(2,1)} %param.16), kind=kOutput, calls=%fused_computation.2 | convolution fusion | flops 4844421120 | bytes 18874368 | tf_op jit(solution)/shard_map/std,df->stf/dot_general | solution.py:743
  146.3 9.6 %multiply_convert_fusion.1 = bf16[2,512,3072]{2,1,0:T(8,128)(2,1)} fusion(bf16[2,512,768]{2,1,0:T(8,128)(2,1)S(1)} %copy-done.4, bf16[2,512,3072]{2,1,0:T(8,128)(2,1)S(1)} %get-tuple-element.149, bf16[2,3072,768]{2,1,0:T(8,128)(2,1)} %param.17), kind=kOutput, calls=%fused_computation.1 | convolution fusion | flops 4850712576 | bytes 18874368 | tf_op jit(solution)/shard_map/std,fd->stf/dot_general | solution.py:786
  155.9 11.8 %weight_grad.23 = bf16[32,96,768]{2,1,0:T(8,128)(2,1)} custom-call(s32[32]{0:T(128)S(1)} %broadcast_select_fusion.22.place_ref, bf16[1024,3072]{1,0:T(8,128)(2,1)} %bitcast.241, bf16[1024,768]{1,0:T(8,128)(2,1)S(1)} %bitcast.197), custom_call_target="tpu_custom_call" | custom-call | flops 4831838208 | bytes 12582912 | tf_op jit(solution)/shard_map/weight_grad/pallas_call | solution.py:609
  167.7 3.3 slice.576
  171.1 9.6 %multiply_reduce_fusion = (f32[768]{0:T(1024)S(1)}, f32[2,512]{1,0:T(2,128)S(1)}, f32[2,512]{1,0:T(2,128)S(1)}, f32[768]{0:T(1024)S(1)}, f32[2,512,768]{2,1,0:T(8,128)S(1)}) fusion(f32[2,512,768]{2,1,0:T(8,128)S(1)} %get-tuple-element.145, f32[2,512]{1,0:T(2,128)S(1)} %add_rsqrt_fusion, f32[2,512]{1,0:T(2,128)S(1)} %broadcast_multiply_fusion.8, ...), kind=kOutput, calls=%fused_computation.60 | convolution fusion | flops 4838912000 | bytes 17327104 | tf_op jit(solution)/shard_map/stf,df->std/dot_general | solution.py:791
  182.7 9.4 %weight_grad.21 = bf16[32,24,3072]{2,1,0:T(8,128)(2,1)} custom-call(s32[32]{0:T(128)S(1)} %broadcast_select_fusion.22.place_ref, bf16[1024,768]{1,0:T(8,128)(2,1)S(1)} %bitcast.208, bf16[1024,3072]{1,0:T(8,128)(2,1)} %bitcast.242), custom_call_target="tpu_custom_call" | custom-call | flops 4831838208 | bytes 12582912 | tf_op jit(solution)/shard_map/weight_grad/pallas_call | solution.py:609
  192.1 3.2 slice.556
  197.0 9.4 %add_convert_fusion.6 = bf16[2,512,768]{2,1,0:T(8,128)(2,1)} fusion(f32[2,512,768]{2,1,0:T(8,128)S(1)} %get-tuple-element.145, bf16[2,512,3072]{2,1,0:T(8,128)(2,1)} %get-tuple-element.148, bf16[2,3072,768]{2,1,0:T(8,128)(2,1)} %param.17), kind=kOutput, calls=%fused_computation.73 | convolution fusion | flops 4833411072 | bytes 15728640 | tf_op jit(solution)/shard_map/stf,fd->std/dot_general | solution.py:746
  210.4 37.7 %attend_back.2 = (bf16[2,3,1024,384]{3,2,1,0:T(8,128)(2,1)}, f32[2,3,3,384]{3,2,1,0:T(4,128)S(1)}) custom-call(s32[2]{0:T(128)S(1)} %copy-done.17, bf16[2,3,1024,384]{3,2,1,0:T(8,128)(2,1)} %get-tuple-element.89.conv_ref, bf16[2,3,1024,384]{3,2,1,0:T(8,128)(2,1)} %get-tuple-element.88.proj_ref, bf16[2,1024,384]{2,1,0:T(8,128)(2,1)S(1)} %convolution_convert_fusion.1.grad_ref, ...), custom_call_target="tpu_custom_call" | custom-call | flops 70000001024 | bytes 16000000 | tf_op jit(solution)/shard_map/attend_back/pallas_call | solution.py:558
  262.1 6.2 %convolution_bitcast_fusion.3 = f32[2,1024,768]{2,1,0:T(8,128)} fusion(bf16[2,3,1024,384]{3,2,1,0:T(8,128)(2,1)S(1)} %bitcast.216, bf16[768,3,768]{0,2,1:T(8,128)(2,1)S(1)} %bitcast.222, s32[]{:T(128)S(6)} %select_n.206), kind=kOutput, calls=%fused_computation.88 | convolution fusion | flops 3623878656 | bytes 12779524 | tf_op jit(solution)/shard_map/sgtc,dgc->std/dot_general | solution.py:812
  294.2 3.6 add_convert_fusion.4
  316.8 6.2 %fusion.85 = (bf16[2,512,768]{2,1,0:T(8,128)(2,1)S(1)}, f32[2,512,768]{2,1,0:T(8,128)S(1)}) fusion(f32[2,512]{1,0:T(2,128)S(1)} %broadcast_multiply_fusion.4, f32[2,512,768]{2,1,0:T(8,128)} %copy-done.18, f32[2,512]{1,0:T(2,128)S(1)} %copy-done.61, f32[2,512]{1,0:T(2,128)S(1)} %broadcast_multiply_fusion.5, f32[2,512,768]{2,1,0:T(8,128)} %get-tuple-element.85, ...), kind=kLoop, calls=%fused_computation.270 | loop fusion | flops 14155776 | bytes 18913280 | tf_op jit(solution)/shard_map/convert_element_type | solution.py:782
  323.0 10.7 %multiply_convert_fusion = bf16[2,512,3072]{2,1,0:T(8,128)(2,1)} fusion(bf16[2,512,768]{2,1,0:T(8,128)(2,1)S(1)} %get-tuple-element.83, bf16[2,512,3072]{2,1,0:T(8,128)(2,1)} %get-tuple-element.141, bf16[2,3072,768]{2,1,0:T(8,128)(2,1)} %param.17), kind=kOutput, calls=%fused_computation | convolution fusion | flops 4850712576 | bytes 18874368 | tf_op jit(solution)/shard_map/std,fd->stf/dot_general | solution.py:786
  333.7 11.8 %weight_grad.22 = bf16[32,96,768]{2,1,0:T(8,128)(2,1)} custom-call(s32[32]{0:T(128)S(1)} %broadcast_select_fusion.22.place_ref, bf16[1024,3072]{1,0:T(8,128)(2,1)} %bitcast.240, bf16[1024,768]{1,0:T(8,128)(2,1)S(1)} %bitcast.206), custom_call_target="tpu_custom_call" | custom-call | flops 4831838208 | bytes 12582912 | tf_op jit(solution)/shard_map/weight_grad/pallas_call | solution.py:609
  345.5 3.4 slice.566
  349.0 9.5 %multiply_reduce_fusion.2 = (f32[768]{0:T(1024)S(1)}, f32[2,512]{1,0:T(2,128)S(1)}, f32[2,512]{1,0:T(2,128)S(1)}, f32[768]{0:T(1024)S(1)}, f32[2,512,768]{2,1,0:T(8,128)S(1)}) fusion(f32[2,512,768]{2,1,0:T(8,128)S(1)} %copy-done.25, f32[2,512]{1,0:T(2,128)S(1)} %copy-done.80, f32[2,512]{1,0:T(2,128)S(1)} %copy-done.73, f32[768]{0:T(1024)S(1)} %copy-done.78, ...), kind=kOutput, calls=%fused_computation.62 | convolution fusion | flops 4838912000 | bytes 17327104 | tf_op jit(solution)/shard_map/stf,df->std/dot_general | solution.py:791
  358.5 9.3 %weight_grad.20 = bf16[32,24,3072]{2,1,0:T(8,128)(2,1)} custom-call(s32[32]{0:T(128)S(1)} %broadcast_select_fusion.22.place_ref, bf16[1024,768]{1,0:T(8,128)(2,1)S(1)} %bitcast.207, bf16[1024,3072]{1,0:T(8,128)(2,1)} %bitcast.243), custom_call_target="tpu_custom_call" | custom-call | flops 4831838208 | bytes 12582912 | tf_op jit(solution)/shard_map/weight_grad/pallas_call | solution.py:609
  367.8 3.3 slice.546
  379.2 5.1 collective-permute-done.15
  387.7 4.7 collective-permute-done.16
  395.7 6.6 %collective-permute-done.48 = bf16[4,96,768]{2,1,0:T(8,128)(2,1)S(1)} collective-permute-done((bf16[4,96,768]{2,1,0:T(8,128)(2,1)S(1)}, bf16[4,96,768]{2,1,0:T(8,128)(2,1)S(1)}, u32[]{:S(2)}, u32[]{:S(2)}) %collective-permute-start.48) | collective-permute-done | bytes 589856 | tf_op jit(solution)/shard_map/ppermute | solution.py:663
  405.3 9.4 %collective-permute-done.49 = bf16[2,96,768]{2,1,0:T(8,128)(2,1)S(1)} collective-permute-done((bf16[2,96,768]{2,1,0:T(8,128)(2,1)S(1)}, bf16[2,96,768]{2,1,0:T(8,128)(2,1)S(1)}, u32[]{:S(2)}, u32[]{:S(2)}) %collective-permute-start.49) | collective-permute-done | bytes 294944 | tf_op jit(solution)/shard_map/ppermute | solution.py:663
  418.0 7.7 %collective-permute-done.50 = bf16[1,96,768]{2,1,0:T(8,128)(2,1)S(1)} collective-permute-done((bf16[1,96,768]{2,1,0:T(8,128)(2,1)S(1)}, bf16[1,96,768]{2,1,0:T(8,128)(2,1)S(1)}, u32[]{:S(2)}, u32[]{:S(2)}) %collective-permute-start.50) | collective-permute-done | bytes 147488 | tf_op jit(solution)/shard_map/ppermute | solution.py:663
  431.4 3.0 weight_grad.18
  437.1 37.6 %attend_back.3 = (bf16[2,3,1024,384]{3,2,1,0:T(8,128)(2,1)}, f32[2,3,3,384]{3,2,1,0:T(4,128)S(1)}) custom-call(s32[2]{0:T(128)S(1)} %copy-done.17, bf16[2,3,1024,384]{3,2,1,0:T(8,128)(2,1)} %get-tuple-element.87.conv_ref, bf16[2,3,1024,384]{3,2,1,0:T(8,128)(2,1)} %get-tuple-element.86.proj_ref, bf16[2,1024,384]{2,1,0:T(8,128)(2,1)S(1)} %convolution_convert_fusion.grad_ref, ...), custom_call_target="tpu_custom_call" | custom-call | flops 70000001024 | bytes 16000000 | tf_op jit(solution)/shard_map/attend_back/pallas_call | solution.py:558
  474.7 8.7 %convolution_bitcast_fusion.2 = f32[2,1024,768]{2,1,0:T(8,128)} fusion(bf16[2,3,1024,384]{3,2,1,0:T(8,128)(2,1)} %get-tuple-element.22, bf16[768,3,768]{0,2,1:T(8,128)(2,1)S(1)} %bitcast.220, s32[]{:T(128)S(6)} %select_n.206), kind=kOutput, calls=%fused_computation.87 | convolution fusion | flops 3623878656 | bytes 12779524 | tf_op jit(solution)/shard_map/sgtc,dgc->std/dot_general | solution.py:812
  496.2 3.5 collective-permute-start.24
  503.9 3.4 collective-permute-done.25
  513.0 3.5 add_convert_fusion.3
  519.1 3.1 add_convert_fusion.5
  536.3 3.9 collective-permute-done.19
  540.3 3.6 collective-permute-done.20
  549.1 7.0 %collective-permute-done.9 = bf16[8,24,2304]{2,1,0:T(8,128)(2,1)S(1)} collective-permute-done((bf16[8,24,2304]{2,1,0:T(8,128)(2,1)S(1)}, bf16[8,24,2304]{2,1,0:T(8,128)(2,1)S(1)}, u32[]{:S(2)}, u32[]{:S(2)}) %collective-permute-start.9) | collective-permute-done | bytes 884768 | tf_op jit(solution)/shard_map/ppermute | solution.py:663
  561.5 4.2 collective-permute-done.10
  580.8 5.9 collective-permute-done.33
  589.7 6.9 %collective-permute-done.34 = bf16[2,24,3072]{2,1,0:T(8,128)(2,1)S(1)} collective-permute-done((bf16[2,24,3072]{2,1,0:T(8,128)(2,1)S(1)}, bf16[2,24,3072]{2,1,0:T(8,128)(2,1)S(1)}, u32[]{:S(2)}, u32[]{:S(2)}) %collective-permute-start.34) | collective-permute-done | bytes 294944 | tf_op jit(solution)/shard_map/ppermute | solution.py:663
  597.9 5.8 collective-permute-done.35
  (511 shorter events, 198.1 us)
Async XLA Ops:
  5.3 13.6 %collective-permute-start = (bf16[2,512,768]{2,1,0:T(8,128)(2,1)S(1)}, bf16[2,512,768]{2,1,0:T(8,128)(2,1)}, u32[]{:S(2)}, u32[]{:S(2)}) collective-permute-start(bf16[2,512,768]{2,1,0:T(8,128)(2,1)S(1)} %fusion.29), channel_id=1, source_target_pairs={{0,16},{16,0},{1,17},{17,1},{2,18},{18,2},{3,19},{19,3},{4,20},{20... | collective-permute-start | bytes 4718600 | tf_op jit(solution)/shard_map/ppermute | solution.py:632
  83.7 6.5 %collective-permute-start.2 = (bf16[2,512,768]{2,1,0:T(8,128)(2,1)}, bf16[2,512,768]{2,1,0:T(8,128)(2,1)}, u32[]{:S(2)}, u32[]{:S(2)}) collective-permute-start(bf16[2,512,768]{2,1,0:T(8,128)(2,1)} %add_convert_fusion.8), channel_id=1, source_target_pairs={{0,16},{16,0},{1,17},{17,1},{2,18},{18,2},{3,19},{19,3},{4,20},{20... | collective-permute-start | bytes 4718600 | tf_op jit(solution)/shard_map/ppermute | solution.py:632
  127.1 5.3 collective-permute-start.3
  182.3 24.1 %collective-permute-start.4 = (bf16[2,512,768]{2,1,0:T(8,128)(2,1)S(1)}, bf16[2,512,768]{2,1,0:T(8,128)(2,1)S(1)}, u32[]{:S(2)}, u32[]{:S(2)}) collective-permute-start(bf16[2,512,768]{2,1,0:T(8,128)(2,1)S(1)} %fusion.83), channel_id=1, source_target_pairs={{0,16},{16,0},{1,17},{17,1},{2,18},{18,2},{3,19},{19,3},{4,20},{20... | collective-permute-start | bytes 4718600 | tf_op jit(solution)/shard_map/ppermute | solution.py:632
  195.4 98.8 %collective-permute-start.36 = (bf16[16,24,3072]{2,1,0:T(8,128)(2,1)}, bf16[16,24,3072]{2,1,0:T(8,128)(2,1)}, u32[]{:S(2)}, u32[]{:S(2)}) collective-permute-start(bf16[16,24,3072]{2,1,0:T(8,128)(2,1)} %slice.556), channel_id=1, source_target_pairs={{0,16},{16,0},{1,17},{17,1},{2,18},{18,2},{3,19},{19,3},{4,20},{20... | collective-permute-start | bytes 7077896 | tf_op jit(solution)/shard_map/ppermute | solution.py:632
  195.5 104.3 %collective-permute-start.46 = (bf16[16,96,768]{2,1,0:T(8,128)(2,1)}, bf16[16,96,768]{2,1,0:T(8,128)(2,1)}, u32[]{:S(2)}, u32[]{:S(2)}) collective-permute-start(bf16[16,96,768]{2,1,0:T(8,128)(2,1)} %slice.576), channel_id=1, source_target_pairs={{0,16},{16,0},{1,17},{17,1},{2,18},{18,2},{3,19},{19,3},{4,20},{20... | collective-permute-start | bytes 7077896 | tf_op jit(solution)/shard_map/ppermute | solution.py:632
  255.9 19.5 %collective-permute-start.27 = (bf16[8,24,768]{2,1,0:T(8,128)(2,1)}, bf16[8,24,768]{2,1,0:T(8,128)(2,1)S(1)}, u32[]{:S(2)}, u32[]{:S(2)}) collective-permute-start(bf16[8,24,768]{2,1,0:T(8,128)(2,1)} %slice.538), channel_id=1, source_target_pairs={{0,1},{1,0},{2,3},{3,2},{4,5},{5,4},{6,7},{7,6},{8,9},{9,8},{10,11... | collective-permute-start | bytes 884744 | tf_op jit(solution)/shard_map/ppermute | solution.py:663
  275.5 5.2 collective-permute-start.28
  281.4 6.6 %collective-permute-start.29 = (bf16[2,24,768]{2,1,0:T(8,128)(2,1)}, bf16[2,24,768]{2,1,0:T(8,128)(2,1)S(1)}, u32[]{:S(2)}, u32[]{:S(2)}) collective-permute-start(bf16[2,24,768]{2,1,0:T(8,128)(2,1)} %slice.542), channel_id=1, source_target_pairs={{0,4},{1,5},{2,6},{3,7},{4,0},{5,1},{6,2},{7,3},{8,12},{9,13},{10,... | collective-permute-start | bytes 221192 | tf_op jit(solution)/shard_map/ppermute | solution.py:663
  287.9 16.9 %collective-permute-start.13 = (bf16[16,24,3,384]{3,1,0,2:T(8,128)(2,1)S(1)}, bf16[16,24,3,384]{3,1,0,2:T(8,128)(2,1)S(1)}, u32[]{:S(2)}, u32[]{:S(2)}) collective-permute-start(bf16[16,24,3,384]{3,1,0,2:T(8,128)(2,1)S(1)} %slice.519), channel_id=1, source_target_pairs={{0,16},{16,0},{1,17},{17,1},{2,18},{18,2},{3,19},{19,3},{4,20},{20... | collective-permute-start | bytes 2654216 | tf_op jit(solution)/shard_map/ppermute | solution.py:632
  288.0 5.5 collective-permute-start.30
  291.5 16.9 %collective-permute-start.5 = (bf16[2,512,768]{2,1,0:T(8,128)(2,1)S(1)}, bf16[2,512,768]{2,1,0:T(8,128)(2,1)S(1)}, u32[]{:S(2)}, u32[]{:S(2)}) collective-permute-start(bf16[2,512,768]{2,1,0:T(8,128)(2,1)S(1)} %dynamic-slice_convert_fusion.1), channel_id=1, source_target_pairs={{0,16},{16,0},{1,17},{17,1},{2,18},{18,2},{3,19},{19,3},{4,20},{20... | collective-permute-start | bytes 4718600 | tf_op jit(solution)/shard_map/ppermute | solution.py:632
  299.0 76.9 %collective-permute-start.37 = (bf16[8,24,3072]{2,1,0:T(8,128)(2,1)}, bf16[8,24,3072]{2,1,0:T(8,128)(2,1)}, u32[]{:S(2)}, u32[]{:S(2)}) collective-permute-start(bf16[8,24,3072]{2,1,0:T(8,128)(2,1)} %slice.558), channel_id=1, source_target_pairs={{0,1},{1,0},{2,3},{3,2},{4,5},{5,4},{6,7},{7,6},{8,9},{9,8},{10,11... | collective-permute-start | bytes 3538952 | tf_op jit(solution)/shard_map/ppermute | solution.py:663
  303.6 82.4 %collective-permute-start.47 = (bf16[8,96,768]{2,1,0:T(8,128)(2,1)}, bf16[8,96,768]{2,1,0:T(8,128)(2,1)}, u32[]{:S(2)}, u32[]{:S(2)}) collective-permute-start(bf16[8,96,768]{2,1,0:T(8,128)(2,1)} %slice.578), channel_id=1, source_target_pairs={{0,1},{1,0},{2,3},{3,2},{4,5},{5,4},{6,7},{7,6},{8,9},{9,8},{10,11... | collective-permute-start | bytes 3538952 | tf_op jit(solution)/shard_map/ppermute | solution.py:663
  306.3 67.9 %collective-permute-start.14 = (bf16[8,24,2304]{2,1,0:T(8,128)(2,1)}, bf16[8,24,2304]{2,1,0:T(8,128)(2,1)}, u32[]{:S(2)}, u32[]{:S(2)}) collective-permute-start(bf16[8,24,2304]{2,1,0:T(8,128)(2,1)} %bitcast.86), channel_id=1, source_target_pairs={{0,1},{1,0},{2,3},{3,2},{4,5},{5,4},{6,7},{7,6},{8,9},{9,8},{10,11... | collective-permute-start | bytes 2654216 | tf_op jit(solution)/shard_map/ppermute | solution.py:663
  348.9 164.1 %collective-permute-start.41 = (bf16[16,96,768]{2,1,0:T(8,128)(2,1)}, bf16[16,96,768]{2,1,0:T(8,128)(2,1)}, u32[]{:S(2)}, u32[]{:S(2)}) collective-permute-start(bf16[16,96,768]{2,1,0:T(8,128)(2,1)} %slice.566), channel_id=1, source_target_pairs={{0,16},{16,0},{1,17},{17,1},{2,18},{18,2},{3,19},{19,3},{4,20},{20... | collective-permute-start | bytes 7077896 | tf_op jit(solution)/shard_map/ppermute | solution.py:632
  371.1 148.0 %collective-permute-start.31 = (bf16[16,24,3072]{2,1,0:T(8,128)(2,1)}, bf16[16,24,3072]{2,1,0:T(8,128)(2,1)}, u32[]{:S(2)}, u32[]{:S(2)}) collective-permute-start(bf16[16,24,3072]{2,1,0:T(8,128)(2,1)} %slice.546), channel_id=1, source_target_pairs={{0,16},{16,0},{1,17},{17,1},{2,18},{18,2},{3,19},{19,3},{4,20},{20... | collective-permute-start | bytes 7077896 | tf_op jit(solution)/shard_map/ppermute | solution.py:632
  374.2 53.9 %collective-permute-start.6 = (bf16[2,512,768]{2,1,0:T(8,128)(2,1)S(1)}, bf16[2,512,768]{2,1,0:T(8,128)(2,1)S(1)}, u32[]{:S(2)}, u32[]{:S(2)}) collective-permute-start(bf16[2,512,768]{2,1,0:T(8,128)(2,1)S(1)} %get-tuple-element.81), channel_id=1, source_target_pairs={{0,16},{16,0},{1,17},{17,1},{2,18},{18,2},{3,19},{19,3},{4,20},{20... | collective-permute-start | bytes 4718600 | tf_op jit(solution)/shard_map/ppermute | solution.py:632
  375.9 8.4 %collective-permute-start.15 = (bf16[4,24,2304]{2,1,0:T(8,128)(2,1)S(1)}, bf16[4,24,2304]{2,1,0:T(8,128)(2,1)S(1)}, u32[]{:S(2)}, u32[]{:S(2)}) collective-permute-start(bf16[4,24,2304]{2,1,0:T(8,128)(2,1)S(1)} %slice.523), channel_id=1, source_target_pairs={{0,2},{1,3},{2,0},{3,1},{4,6},{5,7},{6,4},{7,5},{8,10},{9,11},{10,... | collective-permute-start | bytes 1327112 | tf_op jit(solution)/shard_map/ppermute | solution.py:663
  384.3 9.9 %collective-permute-start.38 = (bf16[4,24,3072]{2,1,0:T(8,128)(2,1)S(1)}, bf16[4,24,3072]{2,1,0:T(8,128)(2,1)S(1)}, u32[]{:S(2)}, u32[]{:S(2)}) collective-permute-start(bf16[4,24,3072]{2,1,0:T(8,128)(2,1)S(1)} %slice.560), channel_id=1, source_target_pairs={{0,2},{1,3},{2,0},{3,1},{4,6},{5,7},{6,4},{7,5},{8,10},{9,11},{10,... | collective-permute-start | bytes 1769480 | tf_op jit(solution)/shard_map/ppermute | solution.py:663
  386.0 6.4 %collective-permute-start.16 = (bf16[2,24,2304]{2,1,0:T(8,128)(2,1)S(1)}, bf16[2,24,2304]{2,1,0:T(8,128)(2,1)S(1)}, u32[]{:S(2)}, u32[]{:S(2)}) collective-permute-start(bf16[2,24,2304]{2,1,0:T(8,128)(2,1)S(1)} %slice.525), channel_id=1, source_target_pairs={{0,4},{1,5},{2,6},{3,7},{4,0},{5,1},{6,2},{7,3},{8,12},{9,13},{10,... | collective-permute-start | bytes 663560 | tf_op jit(solution)/shard_map/ppermute | solution.py:663
  392.4 9.9 %collective-permute-start.48 = (bf16[4,96,768]{2,1,0:T(8,128)(2,1)S(1)}, bf16[4,96,768]{2,1,0:T(8,128)(2,1)S(1)}, u32[]{:S(2)}, u32[]{:S(2)}) collective-permute-start(bf16[4,96,768]{2,1,0:T(8,128)(2,1)S(1)} %slice.580), channel_id=1, source_target_pairs={{0,2},{1,3},{2,0},{3,1},{4,6},{5,7},{6,4},{7,5},{8,10},{9,11},{10,... | collective-permute-start | bytes 1769480 | tf_op jit(solution)/shard_map/ppermute | solution.py:663
  394.1 8.6 %collective-permute-start.17 = (bf16[1,24,2304]{2,1,0:T(8,128)(2,1)S(1)}, bf16[1,24,2304]{2,1,0:T(8,128)(2,1)S(1)}, u32[]{:S(2)}, u32[]{:S(2)}) collective-permute-start(bf16[1,24,2304]{2,1,0:T(8,128)(2,1)S(1)} %slice.527), channel_id=1, source_target_pairs={{0,8},{1,9},{2,10},{3,11},{4,12},{5,13},{6,14},{7,15},{8,0},{9,1},... | collective-permute-start | bytes 331784 | tf_op jit(solution)/shard_map/ppermute | solution.py:663
  402.3 14.1 %collective-permute-start.39 = (bf16[2,24,3072]{2,1,0:T(8,128)(2,1)S(1)}, bf16[2,24,3072]{2,1,0:T(8,128)(2,1)S(1)}, u32[]{:S(2)}, u32[]{:S(2)}) collective-permute-start(bf16[2,24,3072]{2,1,0:T(8,128)(2,1)S(1)} %slice.562), channel_id=1, source_target_pairs={{0,4},{1,5},{2,6},{3,7},{4,0},{5,1},{6,2},{7,3},{8,12},{9,13},{10,... | collective-permute-start | bytes 884744 | tf_op jit(solution)/shard_map/ppermute | solution.py:663
  402.8 12.0 %collective-permute-start.49 = (bf16[2,96,768]{2,1,0:T(8,128)(2,1)S(1)}, bf16[2,96,768]{2,1,0:T(8,128)(2,1)S(1)}, u32[]{:S(2)}, u32[]{:S(2)}) collective-permute-start(bf16[2,96,768]{2,1,0:T(8,128)(2,1)S(1)} %slice.582), channel_id=1, source_target_pairs={{0,4},{1,5},{2,6},{3,7},{4,0},{5,1},{6,2},{7,3},{8,12},{9,13},{10,... | collective-permute-start | bytes 884744 | tf_op jit(solution)/shard_map/ppermute | solution.py:663
  414.8 10.9 %collective-permute-start.50 = (bf16[1,96,768]{2,1,0:T(8,128)(2,1)S(1)}, bf16[1,96,768]{2,1,0:T(8,128)(2,1)S(1)}, u32[]{:S(2)}, u32[]{:S(2)}) collective-permute-start(bf16[1,96,768]{2,1,0:T(8,128)(2,1)S(1)} %slice.584), channel_id=1, source_target_pairs={{0,8},{1,9},{2,10},{3,11},{4,12},{5,13},{6,14},{7,15},{8,0},{9,1},... | collective-permute-start | bytes 442376 | tf_op jit(solution)/shard_map/ppermute | solution.py:663
  416.4 10.9 %collective-permute-start.40 = (bf16[1,24,3072]{2,1,0:T(8,128)(2,1)S(1)}, bf16[1,24,3072]{2,1,0:T(8,128)(2,1)S(1)}, u32[]{:S(2)}, u32[]{:S(2)}) collective-permute-start(bf16[1,24,3072]{2,1,0:T(8,128)(2,1)S(1)} %slice.564), channel_id=1, source_target_pairs={{0,8},{1,9},{2,10},{3,11},{4,12},{5,13},{6,14},{7,15},{8,0},{9,1},... | collective-permute-start | bytes 442376 | tf_op jit(solution)/shard_map/ppermute | solution.py:663
  436.0 59.1 %collective-permute-start.23 = (bf16[8,24,768]{2,1,0:T(8,128)(2,1)}, bf16[8,24,768]{2,1,0:T(8,128)(2,1)}, u32[]{:S(2)}, u32[]{:S(2)}) collective-permute-start(bf16[8,24,768]{2,1,0:T(8,128)(2,1)} %slice.530), channel_id=1, source_target_pairs={{0,1},{1,0},{2,3},{3,2},{4,5},{5,4},{6,7},{7,6},{8,9},{9,8},{10,11... | collective-permute-start | bytes 884744 | tf_op jit(solution)/shard_map/ppermute | solution.py:663
  496.2 6.6 %collective-permute-start.24 = (bf16[4,24,768]{2,1,0:T(8,128)(2,1)S(1)}, bf16[4,24,768]{2,1,0:T(8,128)(2,1)S(1)}, u32[]{:S(2)}, u32[]{:S(2)}) collective-permute-start(bf16[4,24,768]{2,1,0:T(8,128)(2,1)S(1)} %slice.532), channel_id=1, source_target_pairs={{0,2},{1,3},{2,0},{3,1},{4,6},{5,7},{6,4},{7,5},{8,10},{9,11},{10,... | collective-permute-start | bytes 442376 | tf_op jit(solution)/shard_map/ppermute | solution.py:663
  502.9 4.4 collective-permute-start.25
  503.9 20.4 %collective-permute-start.8 = (bf16[16,24,3,384]{3,1,0,2:T(8,128)(2,1)S(1)}, bf16[16,24,3,384]{3,1,0,2:T(8,128)(2,1)S(1)}, u32[]{:S(2)}, u32[]{:S(2)}) collective-permute-start(bf16[16,24,3,384]{3,1,0,2:T(8,128)(2,1)S(1)} %slice.509), channel_id=1, source_target_pairs={{0,16},{16,0},{1,17},{17,1},{2,18},{18,2},{3,19},{19,3},{4,20},{20... | collective-permute-start | bytes 2654216 | tf_op jit(solution)/shard_map/ppermute | solution.py:632
  507.3 4.9 collective-permute-start.26
  510.4 15.3 %collective-permute-start.7 = (bf16[2,512,768]{2,1,0:T(8,128)(2,1)S(1)}, bf16[2,512,768]{2,1,0:T(8,128)(2,1)S(1)}, u32[]{:S(2)}, u32[]{:S(2)}) collective-permute-start(bf16[2,512,768]{2,1,0:T(8,128)(2,1)S(1)} %dynamic-slice_convert_fusion), channel_id=1, source_target_pairs={{0,16},{16,0},{1,17},{17,1},{2,18},{18,2},{3,19},{19,3},{4,20},{20... | collective-permute-start | bytes 4718600 | tf_op jit(solution)/shard_map/ppermute | solution.py:632
  517.6 49.6 %collective-permute-start.42 = (bf16[8,96,768]{2,1,0:T(8,128)(2,1)}, bf16[8,96,768]{2,1,0:T(8,128)(2,1)}, u32[]{:S(2)}, u32[]{:S(2)}) collective-permute-start(bf16[8,96,768]{2,1,0:T(8,128)(2,1)} %slice.568), channel_id=1, source_target_pairs={{0,1},{1,0},{2,3},{3,2},{4,5},{5,4},{6,7},{7,6},{8,9},{9,8},{10,11... | collective-permute-start | bytes 3538952 | tf_op jit(solution)/shard_map/ppermute | solution.py:663
  523.3 51.8 %collective-permute-start.32 = (bf16[8,24,3072]{2,1,0:T(8,128)(2,1)}, bf16[8,24,3072]{2,1,0:T(8,128)(2,1)}, u32[]{:S(2)}, u32[]{:S(2)}) collective-permute-start(bf16[8,24,3072]{2,1,0:T(8,128)(2,1)} %slice.548), channel_id=1, source_target_pairs={{0,1},{1,0},{2,3},{3,2},{4,5},{5,4},{6,7},{7,6},{8,9},{9,8},{10,11... | collective-permute-start | bytes 3538952 | tf_op jit(solution)/shard_map/ppermute | solution.py:663
  533.6 22.5 %collective-permute-start.9 = (bf16[8,24,2304]{2,1,0:T(8,128)(2,1)S(1)}, bf16[8,24,2304]{2,1,0:T(8,128)(2,1)S(1)}, u32[]{:S(2)}, u32[]{:S(2)}) collective-permute-start(bf16[8,24,2304]{2,1,0:T(8,128)(2,1)S(1)} %bitcast.225), channel_id=1, source_target_pairs={{0,1},{1,0},{2,3},{3,2},{4,5},{5,4},{6,7},{7,6},{8,9},{9,8},{10,11... | collective-permute-start | bytes 2654216 | tf_op jit(solution)/shard_map/ppermute | solution.py:663
  534.8 5.3 collective-permute-start.19
  544.0 3.8 collective-permute-start.21
  547.8 11.2 %collective-permute-start.22 = (f32[1,2,312]{2,0,1:T(1,128)S(1)}, f32[1,2,312]{2,0,1:T(1,128)S(1)}, u32[]{:S(2)}, u32[]{:S(2)}) collective-permute-start(f32[1,2,312]{2,0,1:T(1,128)S(1)} %constant_dynamic-slice_fusion), channel_id=1, source_target_pairs={{0,1},{1,0},{2,3},{3,2},{4,5},{5,4},{6,7},{7,6},{8,9},{9,8},{10,11... | collective-permute-start | bytes 7496 | tf_op jit(solution)/shard_map/ppermute | solution.py:884
  557.0 8.6 %collective-permute-start.10 = (bf16[4,24,2304]{2,1,0:T(8,128)(2,1)}, bf16[4,24,2304]{2,1,0:T(8,128)(2,1)}, u32[]{:S(2)}, u32[]{:S(2)}) collective-permute-start(bf16[4,24,2304]{2,1,0:T(8,128)(2,1)} %slice.513), channel_id=1, source_target_pairs={{0,2},{1,3},{2,0},{3,1},{4,6},{5,7},{6,4},{7,5},{8,10},{9,11},{10,... | collective-permute-start | bytes 1327112 | tf_op jit(solution)/shard_map/ppermute | solution.py:663
  566.8 6.0 collective-permute-start.11
  569.0 10.8 %collective-permute-start.43 = (bf16[4,96,768]{2,1,0:T(8,128)(2,1)S(1)}, bf16[4,96,768]{2,1,0:T(8,128)(2,1)S(1)}, u32[]{:S(2)}, u32[]{:S(2)}) collective-permute-start(bf16[4,96,768]{2,1,0:T(8,128)(2,1)S(1)} %slice.570), channel_id=1, source_target_pairs={{0,2},{1,3},{2,0},{3,1},{4,6},{5,7},{6,4},{7,5},{8,10},{9,11},{10,... | collective-permute-start | bytes 1769480 | tf_op jit(solution)/shard_map/ppermute | solution.py:663
  572.9 6.9 %collective-permute-start.12 = (bf16[1,24,2304]{2,1,0:T(8,128)(2,1)S(1)}, bf16[1,24,2304]{2,1,0:T(8,128)(2,1)S(1)}, u32[]{:S(2)}, u32[]{:S(2)}) collective-permute-start(bf16[1,24,2304]{2,1,0:T(8,128)(2,1)S(1)} %slice.517), channel_id=1, source_target_pairs={{0,8},{1,9},{2,10},{3,11},{4,12},{5,13},{6,14},{7,15},{8,0},{9,1},... | collective-permute-start | bytes 331784 | tf_op jit(solution)/shard_map/ppermute | solution.py:663
  576.7 9.9 %collective-permute-start.33 = (bf16[4,24,3072]{2,1,0:T(8,128)(2,1)S(1)}, bf16[4,24,3072]{2,1,0:T(8,128)(2,1)S(1)}, u32[]{:S(2)}, u32[]{:S(2)}) collective-permute-start(bf16[4,24,3072]{2,1,0:T(8,128)(2,1)S(1)} %slice.550), channel_id=1, source_target_pairs={{0,2},{1,3},{2,0},{3,1},{4,6},{5,7},{6,4},{7,5},{8,10},{9,11},{10,... | collective-permute-start | bytes 1769480 | tf_op jit(solution)/shard_map/ppermute | solution.py:663
  580.0 8.6 %collective-permute-start.44 = (bf16[2,96,768]{2,1,0:T(8,128)(2,1)S(1)}, bf16[2,96,768]{2,1,0:T(8,128)(2,1)S(1)}, u32[]{:S(2)}, u32[]{:S(2)}) collective-permute-start(bf16[2,96,768]{2,1,0:T(8,128)(2,1)S(1)} %slice.572), channel_id=1, source_target_pairs={{0,4},{1,5},{2,6},{3,7},{4,0},{5,1},{6,2},{7,3},{8,12},{9,13},{10,... | collective-permute-start | bytes 884744 | tf_op jit(solution)/shard_map/ppermute | solution.py:663
  586.8 9.8 %collective-permute-start.34 = (bf16[2,24,3072]{2,1,0:T(8,128)(2,1)S(1)}, bf16[2,24,3072]{2,1,0:T(8,128)(2,1)S(1)}, u32[]{:S(2)}, u32[]{:S(2)}) collective-permute-start(bf16[2,24,3072]{2,1,0:T(8,128)(2,1)S(1)} %slice.552), channel_id=1, source_target_pairs={{0,4},{1,5},{2,6},{3,7},{4,0},{5,1},{6,2},{7,3},{8,12},{9,13},{10,... | collective-permute-start | bytes 884744 | tf_op jit(solution)/shard_map/ppermute | solution.py:663
  588.8 8.3 %collective-permute-start.45 = (bf16[1,96,768]{2,1,0:T(8,128)(2,1)S(1)}, bf16[1,96,768]{2,1,0:T(8,128)(2,1)S(1)}, u32[]{:S(2)}, u32[]{:S(2)}) collective-permute-start(bf16[1,96,768]{2,1,0:T(8,128)(2,1)S(1)} %slice.574), channel_id=1, source_target_pairs={{0,8},{1,9},{2,10},{3,11},{4,12},{5,13},{6,14},{7,15},{8,0},{9,1},... | collective-permute-start | bytes 442376 | tf_op jit(solution)/shard_map/ppermute | solution.py:663
  596.7 7.0 %collective-permute-start.35 = (bf16[1,24,3072]{2,1,0:T(8,128)(2,1)S(1)}, bf16[1,24,3072]{2,1,0:T(8,128)(2,1)S(1)}, u32[]{:S(2)}, u32[]{:S(2)}) collective-permute-start(bf16[1,24,3072]{2,1,0:T(8,128)(2,1)S(1)} %slice.554), channel_id=1, source_target_pairs={{0,8},{1,9},{2,10},{3,11},{4,12},{5,13},{6,14},{7,15},{8,0},{9,1},... | collective-permute-start | bytes 442376 | tf_op jit(solution)/shard_map/ppermute | solution.py:663
  (108 other events, 938.6 us)
